TPU v7x, 256 devices: a whole 4x4x8 slice. The times are simulated.
256 devices in a mesh: freq: 8 (over z_hi, y), sy: 8 (over z_lo, core), sx: 4 (over x).
Axes of the slice: x: 4, y: 4, z: 8 (z_hi: 2, z_lo: 4; z = z_hi * 4 + z_lo), core: 2. Of those that a mesh axis runs over, the one named last changes fastest.
Arguments:
- cube: bfloat16 [1024, 128, 512], P('freq', 'sy', 'sx')
- pos_embed: bfloat16 [1024, 768], replicated, may hold values from -3 to 3
- w_in: bfloat16 [256, 768], replicated, may hold values from -0.375 to 0.375
- norm_gain: float32 [768], replicated, may hold values from 0.5 to 1.5
- w_query: bfloat16 [768, 768], replicated, may hold values from -0.21875 to 0.21875
- w_key: bfloat16 [768, 768], replicated, may hold values from -0.21875 to 0.21875
- w_value: bfloat16 [768, 768], replicated, may hold values from -0.21875 to 0.21875
- w_out: bfloat16 [768, 768], replicated, may hold values from -0.21875 to 0.21875
- attn_scale: float32 [12], replicated, may hold values from 3 to 30
- w_proj: bfloat16 [768, 512], replicated, may hold values from -0.21875 to 0.21875
- mix_weight: float32 [3, 3, 512], replicated, may hold values from -2 to 2
- optical: bfloat16 [1024, 512], P(('freq', 'sy', 'sx'))
- logit_scale: float32 [1], replicated, may hold values from 40 to 50
- pattern: int32 [8, 4, 8, 8, 3], P('sy', 'sx', 'freq'), may hold values from 0 to 7, as said below
- match_ids: int32 [8, 4, 8], P('sy', 'sx', 'freq'), may hold values from 0 to 1023, as said below
Outputs:
- layer_out: bfloat16 [8, 4, 8, 1024, 768], P('sy', 'sx', 'freq')
- embed: float32 [8, 4, 8, 512], P('sy', 'sx', 'freq')
- block_loss: float32 [8, 4, 8], P('sy', 'sx', 'freq')
Inputs may be any that keep to these rules, and one draw needn't show every extreme that they name: `pattern`: for every pixel block and query block, the 3 key block indices are distinct. `match_ids`: counting devices on freq+sy+sx with freq slowest, the block of device d = f * 8 * 4 + i * 4 + j has its counterpart among the 4 candidates of device (d + 128) mod 256.
All inputs are finite; a program needn't handle non-finite values.
Results may differ from a plain program's by a relative error of at most 0.012.
The roundings to bfloat16 on the way count: a program that leaves them out, or rounds other values in their place, can miss the bound.
Values may be sent and summed in bfloat16 or wider, within the bound.
No kernel may reach another device: no remote copies, remote signals or barrier semaphores. Data moves between devices by JAX's collectives and lax.ppermute only.
A program may use at most 128 MiB of HBM per device.

v0:
```python
import jax
import jax.numpy as jnp
from jax import lax
from jax.sharding import PartitionSpec as P

LB = 128
KSEL = 3
HEADS = 12
HD = 64


def passed_along(array, axis, by):
    peers = lax.axis_size(axis)
    return lax.ppermute(array, axis, [(i, (i + by) % peers) for i in range(peers)])


def padded_2(array, sides, width):
    for axis, dim in sides:
        peers, length = (lax.axis_size(axis), array.shape[dim])
        up = [(i, (i + 1) % peers) for i in range(peers - 1)]
        down = [(j, i) for i, j in up]
        last = lax.slice_in_dim(array, length - width, length, axis=dim)
        initial = lax.slice_in_dim(array, 0, width, axis=dim)
        before = lax.ppermute(last, axis, up)
        after = lax.ppermute(initial, axis, down)
        array = jnp.concatenate([before, array, after], axis=dim)
    return array


def attention_layer(
    spectra, choose, pos_embed, w_in, norm_gain, w_query, w_key, w_value, w_out, attn_scale
):
    values = spectra.astype(jnp.float32)
    centre = jnp.mean(values, axis=0)
    spread = jnp.mean(jnp.square(values - centre), axis=0)
    unit_spec = ((values - centre) * lax.rsqrt(spread + 1e-05)).astype(jnp.bfloat16)
    tokens = jnp.dot(unit_spec, w_in, preferred_element_type=jnp.float32) + pos_embed.astype(
        jnp.float32
    )
    square_mean = jnp.mean(tokens * tokens, axis=-1, keepdims=True)
    normed = (tokens * lax.rsqrt(square_mean + 1e-06) * norm_gain).astype(jnp.bfloat16)
    channels = tokens.shape[0]
    nblocks = channels // LB

    def unit_heads(weight):
        projected = jnp.dot(normed, weight, preferred_element_type=jnp.float32).reshape(
            channels, HEADS, HD
        )
        length = jnp.sum(projected * projected, axis=-1, keepdims=True)
        return (
            (projected * lax.rsqrt(length + 1e-06))
            .astype(jnp.bfloat16)
            .reshape(nblocks, LB, HEADS, HD)
        )

    queries = unit_heads(w_query)
    key_blocks = unit_heads(w_key)
    value_blocks = (
        jnp.dot(normed, w_value, preferred_element_type=jnp.float32)
        .astype(jnp.bfloat16)
        .reshape(nblocks, LB, HEADS, HD)
    )
    chosen_keys = jnp.take(key_blocks, choose, axis=0).reshape(nblocks, KSEL * LB, HEADS, HD)
    chosen_values = jnp.take(value_blocks, choose, axis=0).reshape(nblocks, KSEL * LB, HEADS, HD)
    scores = jnp.einsum("qlhd,qmhd->qhlm", queries, chosen_keys, preferred_element_type=jnp.float32)
    scores = scores * attn_scale[None, :, None, None]
    highest = jnp.max(scores, axis=-1, keepdims=True)
    weights = jnp.exp(scores - highest)
    probs = (weights / jnp.sum(weights, axis=-1, keepdims=True)).astype(jnp.bfloat16)
    heads_out = jnp.einsum(
        "qhlm,qmhd->qlhd", probs, chosen_values, preferred_element_type=jnp.float32
    )
    heads_out = heads_out.astype(jnp.bfloat16).reshape(channels, HEADS * HD)
    return tokens + jnp.dot(heads_out, w_out, preferred_element_type=jnp.float32)


def per_device(
    cube,
    pos_embed,
    w_in,
    norm_gain,
    w_query,
    w_key,
    w_value,
    w_out,
    attn_scale,
    w_proj,
    mix_weight,
    optical,
    logit_scale,
    pattern,
    match_ids,
):
    nfreq = lax.axis_size("freq")
    local_chans = cube.shape[0]
    side = cube.shape[1]
    planes = (
        cube.reshape(local_chans, side, nfreq, side)
        .transpose(2, 0, 1, 3)
        .reshape(nfreq, local_chans, side * side)
    )
    spectra = lax.all_to_all(planes, "freq", split_axis=0, concat_axis=1, tiled=True)[0]
    choose = pattern.reshape(pattern.shape[3], pattern.shape[4])
    layer = attention_layer(
        spectra, choose, pos_embed, w_in, norm_gain, w_query, w_key, w_value, w_out, attn_scale
    )
    layer_out = layer.astype(jnp.bfloat16).reshape(1, 1, 1, layer.shape[0], layer.shape[1])
    pooled = jnp.mean(layer, axis=0).astype(jnp.bfloat16)
    projected = jnp.dot(pooled[None, :], w_proj, preferred_element_type=jnp.float32)
    lower_piece = passed_along(projected, "freq", 1)
    upper_piece = passed_along(projected, "freq", -1)
    strip = jnp.concatenate([upper_piece, projected, lower_piece], axis=0)[None]
    padded = padded_2(strip, (("sy", 0), ("sx", 1)), 1)
    column = lax.axis_index("freq")
    left_side = jnp.where(column == 0, padded[:, 0], padded[:, 3])
    right_side = jnp.where(column == nfreq - 1, padded[:, 4], padded[:, 1])
    window = jnp.stack([left_side, padded[:, 2], right_side], axis=1)
    mixed = jnp.sum(window * mix_weight, axis=(0, 1))
    embed = mixed.reshape(1, 1, 1, mixed.shape[0])
    unit = (mixed * lax.rsqrt(jnp.sum(mixed * mixed) + 1e-06)).astype(jnp.bfloat16)
    optical_f = optical.astype(jnp.float32)
    optical_unit = (
        optical_f * lax.rsqrt(jnp.sum(optical_f * optical_f, axis=-1, keepdims=True) + 1e-06)
    ).astype(jnp.bfloat16)
    scale = logit_scale[0]
    target = match_ids.reshape(())
    start_carry = (
        jnp.full((), -jnp.inf, jnp.float32),
        jnp.zeros((), jnp.float32),
        jnp.zeros((), jnp.float32),
    )
    piece = lax.all_gather(optical_unit, ("freq", "sy", "sx"), axis=0, tiled=True)
    logits = jnp.dot(piece, unit, preferred_element_type=jnp.float32) * scale
    highest = jnp.max(logits)
    summed = start_carry[1] * jnp.exp(start_carry[0] - highest) + jnp.sum(jnp.exp(logits - highest))
    positions = jnp.arange(piece.shape[0], dtype=jnp.int32)
    positive = jnp.sum(jnp.where(positions == target, logits, 0.0))
    highest, summed, positive = (highest, summed, positive)
    loss = jnp.log(summed) + highest - positive
    return (layer_out, embed, loss.reshape(1, 1, 1))


def solution(mesh):
    in_specs = (
        P("freq", "sy", "sx"),
        P(),
        P(),
        P(),
        P(),
        P(),
        P(),
        P(),
        P(),
        P(),
        P(),
        P(("freq", "sy", "sx"), None),
        P(),
        P("sy", "sx", "freq", None, None),
        P("sy", "sx", "freq"),
    )
    out_specs = (
        P("sy", "sx", "freq", None, None),
        P("sy", "sx", "freq", None),
        P("sy", "sx", "freq"),
    )
    return jax.shard_map(
        per_device, mesh=mesh, in_specs=in_specs, out_specs=out_specs, check_vma=False
    )
```

profile of v0, /device:TPU:3, one launch (start us, length us, event | category | flops | bytes accessed | tf_op | source)
XLA Modules:
  0.0 568.9 jit_solution(14749514840353726318)
XLA Ops:
  7.2 1.6 copy.55
  9.6 10.8 %all-to-all-start = ((bf16[8,128,256]{1,2,0:T(8,128)(2,1)}), bf16[8,128,256]{1,2,0:T(8,128)(2,1)S(1)}, u32[]{:S(2)}, u32[]{:S(2)}) async-start(bf16[8,128,256]{1,2,0:T(8,128)(2,1)} %bitcast.2), calls=%async_computation | async-start | bytes 1048576 | tf_op jit(solution)/shard_map/all_to_all | solution.py:102
  21.6 10.4 %all-to-all-done = bf16[8,128,256]{1,2,0:T(8,128)(2,1)S(1)} async-done(((bf16[8,128,256]{1,2,0:T(8,128)(2,1)}), bf16[8,128,256]{1,2,0:T(8,128)(2,1)S(1)}, u32[]{:S(2)}, u32[]{:S(2)}) %all-to-all-start) | async-done | bytes 524320 | tf_op jit(solution)/shard_map/all_to_all | solution.py:102
  32.8 2.1 multiply_reduce_fusion.1
  34.9 1.7 copy-done.4
  37.0 3.1 fusion.39
  40.1 2.4 copy.77
  42.5 2.3 reduce_sum.112
  44.9 3.8 convolution_convert_fusion
  48.7 1.7 copy.59
  51.3 1.0 copy-done.6
  53.1 3.5 gather_fusion.1
  56.6 3.4 gather_fusion
  60.0 4.3 fusion.40
  65.1 2.3 reduce_sum.111
  67.4 6.8 %select_bitcast_fusion.1 = (bf16[8,3,12,8,8,128]{5,4,3,2,1,0:T(8,128)(2,1)}, bf16[8,3,12,8,8,128]{5,4,3,2,1,0:T(8,128)(2,1)S(1)}) fusion(bf16[8,3,128,12,64]{2,4,3,1,0:T(8,128)(2,1)} %bitcast.99, pred[8,3]{1,0:T(8,128)(4,1)S(1)} %copy.58, bf16[8,3,128,12,64]{2,4,3,1,0:T(8,128)(2,1)} %bitcast.98), kind=kLoop, calls=%fused_computation.15 | loop fusion | flops 4718592 | bytes 18874392
  74.3 7.9 %fusion.6 = f32[8,12,128,384]{3,2,1,0:T(8,128)} fusion(bf16[8,3,12,8,8,128]{5,4,3,2,1,0:T(8,128)(2,1)S(1)} %get-tuple-element.11, f32[8,128,12,64]{1,0,3,2:T(8,128)S(1)} %bitcast.100, f32[8,128,12]{1,2,0:T(8,128)S(1)} %copy.63), kind=kOutput, calls=%fused_computation.9 | convolution fusion | flops 605552640 | bytes 26787840 | tf_op jit(solution)/shard_map/qlhd,qmhd->qhlm/dot_general | solution.py:65
  82.2 15.6 %fusion.41 = f32[8,12,128]{2,1,0:T(8,128)S(1)} fusion(f32[8,12,128,384]{3,2,1,0:T(8,128)} %fusion.6, f32[12]{0:T(128)S(1)} %copy-done.15), kind=kOutput, calls=%fused_computation.78 | output fusion | flops 18874752 | bytes 18923568 | tf_op jit(solution)/shard_map/sub | solution.py:68
  97.8 27.8 %fusion.20 = bf16[8,128,12,64]{1,3,2,0:T(8,128)(2,1)S(1)} fusion(f32[8,12,128]{2,1,0:T(8,128)S(1)} %fusion.41, bf16[8,3,12,8,8,128]{5,4,3,2,1,0:T(8,128)(2,1)} %get-tuple-element.10, f32[8,12,128,384]{3,2,1,0:T(8,128)} %fusion.6, f32[12]{0:T(128)S(1)} %copy-done.15), kind=kOutput, calls=%fused_computation.30 | convolution fusion | flops 628371840 | bytes 25215024 | tf_op jit(solution)/shard_map/qhlm,qmhd->qlhd/dot_general | solution.py:70
  125.7 1.2 copy.70
  127.5 2.7 fusion.38
  130.5 3.9 collective-permute-start
  135.1 7.7 %collective-permute-done.1 = f32[1,512]{1,0:T(1,128)S(1)} collective-permute-done((f32[1,512]{1,0:T(1,128)S(1)}, f32[1,512]{1,0:T(1,128)S(1)}, u32[]{:S(2)}, u32[]{:S(2)}) %collective-permute-start.1) | collective-permute-done | bytes 2080 | tf_op jit(solution)/shard_map/ppermute | solution.py:14
  142.8 9.4 %collective-permute-start.2 = (f32[1,3,512]{2,1,0:T(4,128)S(1)}, f32[1,3,512]{2,1,0:T(4,128)S(1)}, u32[]{:S(2)}, u32[]{:S(2)}) collective-permute-start(f32[1,3,512]{2,1,0:T(4,128)S(1)} %maximum_bitcast_fusion), channel_id=1, source_target_pairs={{0,4},{4,8},{8,12},{12,16},{16,20},{20,24},{24,28},{1,5},{5,9},{9,... | collective-permute-start | bytes 18440 | tf_op jit(solution)/shard_map/ppermute | solution.py:24
  152.2 1.9 collective-permute-start.3
  154.1 3.0 collective-permute-done.3
  157.2 3.1 collective-permute-start.4
  161.6 2.2 collective-permute-start.5
  163.8 2.2 collective-permute-done.5
  167.4 387.2 %all-gather.3.cloned.1.call-done = bf16[256,4,512]{2,1,0:T(4,128)(2,1)} async-done(((bf16[1,4,512]{2,1,0:T(4,128)(2,1)}), bf16[256,4,512]{2,1,0:T(4,128)(2,1)}) %all-gather.3.cloned.1.call-update) | async-done | bytes 1048592 | tf_op jit(solution)/shard_map/all_gather | solution.py:132
  554.6 1.3 reshape.161
  557.6 1.3 select_reduce_fusion
  (79 shorter events, 8.8 us)
Async XLA Ops:
  7.2 29.8 %copy-start = (bf16[768,768]{1,0:T(8,128)(2,1)S(1)}, bf16[768,768]{1,0:T(8,128)(2,1)}, u32[]{:S(2)}) copy-start(bf16[768,768]{1,0:T(8,128)(2,1)} %param.22) | copy-start | bytes 3538948
  7.2 13.3 %copy-start.11 = (bf16[4,512]{1,0:T(4,128)(2,1)S(1)}, bf16[4,512]{1,0:T(4,128)(2,1)}, u32[]{:S(2)}) copy-start(bf16[4,512]{1,0:T(4,128)(2,1)} %param.28) | copy-start | bytes 12292
  7.2 14.1 %copy-start.12 = (s32[1,1,1,8,3]{3,2,4,1,0:T(1,128)S(1)}, s32[1,1,1,8,3]{3,2,4,1,0:T(1,128)}, u32[]{:S(2)}) copy-start(s32[1,1,1,8,3]{3,2,4,1,0:T(1,128)} %param.30) | copy-start | bytes 292
  8.8 24.0 %copy-start.8 = (bf16[256,768]{1,0:T(8,128)(2,1)S(1)}, bf16[256,768]{1,0:T(8,128)(2,1)}, u32[]{:S(2)}) copy-start(bf16[256,768]{1,0:T(8,128)(2,1)} %param.19) | copy-start | bytes 1179652
  9.6 22.4 %all-to-all-start = ((bf16[8,128,256]{1,2,0:T(8,128)(2,1)}), bf16[8,128,256]{1,2,0:T(8,128)(2,1)S(1)}, u32[]{:S(2)}, u32[]{:S(2)}) async-start(bf16[8,128,256]{1,2,0:T(8,128)(2,1)} %bitcast.2), calls=%async_computation | async-start | bytes 1048576 | tf_op jit(solution)/shard_map/all_to_all | solution.py:102
  20.4 534.2 %all-gather.3.cloned.1.call-start = ((), (), s32[]{:S(2)}) async-start(), calls=%async_computation.1 | async-start | bytes 1052672 | tf_op jit(solution)/shard_map/all_gather | solution.py:132
  32.8 3.8 copy-start.13
  34.9 1.7 copy-start.4
  37.0 7.9 %copy-start.2 = (bf16[1024,768]{1,0:T(8,128)(2,1)}, bf16[1024,768]{1,0:T(8,128)(2,1)S(1)}, u32[]{:S(2)}) copy-start(bf16[1024,768]{1,0:T(8,128)(2,1)S(1)} %multiply_convert_fusion) | copy-start | bytes 4718596
  50.4 1.9 copy-start.6
  56.5 3.4 copy-start.3
  74.3 7.9 %copy-start.15 = (f32[12]{0:T(128)S(1)}, f32[12]{0:T(128)}, u32[]{:S(2)}) copy-start(f32[12]{0:T(128)} %param.25) | copy-start | bytes 148
  97.8 29.1 %copy-start.14 = (bf16[768,768]{1,0:T(8,128)(2,1)S(1)}, bf16[768,768]{1,0:T(8,128)(2,1)}, u32[]{:S(2)}) copy-start(bf16[768,768]{1,0:T(8,128)(2,1)} %param.24) | copy-start | bytes 3538948
  125.6 1.9 copy-start.5
  127.5 2.7 copy-start.7
  127.5 38.5 %copy-start.9 = (f32[3,3,512]{2,1,0:T(4,128)S(1)}, f32[3,3,512]{2,1,0:T(4,128)}, u32[]{:S(2)}) copy-start(f32[3,3,512]{2,1,0:T(4,128)} %param.27) | copy-start | bytes 55300
  127.5 433.3 %copy-start.1 = (bf16[768,768]{1,0:T(8,128)(2,1)S(1)}, bf16[768,768]{1,0:T(8,128)(2,1)}, u32[]{:S(2)}) copy-start(bf16[768,768]{1,0:T(8,128)(2,1)} %param.22) | copy-start | bytes 3538948
  130.5 4.6 collective-permute-start
  134.3 8.5 %collective-permute-start.1 = (f32[1,512]{1,0:T(1,128)S(1)}, f32[1,512]{1,0:T(1,128)S(1)}, u32[]{:S(2)}, u32[]{:S(2)}) collective-permute-start(f32[1,512]{1,0:T(1,128)S(1)} %fusion.44), channel_id=1, source_target_pairs={{0,32},{32,64},{64,96},{96,128},{128,160},{160,192},{192,224},{224... | collective-permute-start | bytes 6152 | tf_op jit(solution)/shard_map/ppermute | solution.py:14
  142.8 11.3 %collective-permute-start.2 = (f32[1,3,512]{2,1,0:T(4,128)S(1)}, f32[1,3,512]{2,1,0:T(4,128)S(1)}, u32[]{:S(2)}, u32[]{:S(2)}) collective-permute-start(f32[1,3,512]{2,1,0:T(4,128)S(1)} %maximum_bitcast_fusion), channel_id=1, source_target_pairs={{0,4},{4,8},{8,12},{12,16},{16,20},{20,24},{24,28},{1,5},{5,9},{9,... | collective-permute-start | bytes 18440 | tf_op jit(solution)/shard_map/ppermute | solution.py:24
  152.2 5.0 collective-permute-start.3
  157.2 6.6 %collective-permute-start.4 = (f32[3,1,512]{2,1,0:T(1,128)S(1)}, f32[3,1,512]{2,1,0:T(1,128)S(1)}, u32[]{:S(2)}, u32[]{:S(2)}) collective-permute-start(f32[3,1,512]{2,1,0:T(1,128)S(1)} %get-tuple-element.8), channel_id=1, source_target_pairs={{0,1},{1,2},{2,3},{4,5},{5,6},{6,7},{8,9},{9,10},{10,11},{12,13},{... | collective-permute-start | bytes 18440 | tf_op jit(solution)/shard_map/ppermute | solution.py:24
  161.6 4.4 collective-permute-start.5
  166.1 394.8 %copy-start.10 = (f32[512]{0:T(512)}, f32[512]{0:T(512)S(1)}, u32[]{:S(2)}) copy-start(f32[512]{0:T(512)S(1)} %fusion.33) | copy-start | bytes 6148
Sparse Core Ops, SparseCore 0:
  23.0 531.4 all-gather.2
where the time goes:
time: 571 us; the launch traced here: 569 us
  waiting for transfers between devices  411 us (72%)
  matrix products  52.3 us (9%)
  other arithmetic  32.2 us (6%)
  starting transfers between devices  31.3 us (5%)
  local copies, waits for them, and re-layouts  21.5 us (4%)
  between operations  20.2 us (4%)
    all_gather x1, waiting for transfers between devices, per_device(): lax.all_gather(optical_unit, ('freq', 'sy', 'sx'), axis=0, tiled=True)  387 us
    dot_general x1, matrix products, attention_layer(): jnp.einsum('qhlm,qmhd->qlhd', probs, chosen_values, preferred_element_typ...  27.8 us
    sub x1, other arithmetic, attention_layer(): weights = jnp.exp(scores - highest)  15.6 us
    ppermute x2, starting transfers between devices, padded_2(): before = lax.ppermute(last, axis, up)  12.5 us
  transfers between devices with their start and end apart: 8, of which 6 were waited for; matrix products, arithmetic and copies ran while one was open for 17% of the time, Pallas kernels for 0%

commit v1 on v0

v1 whole, which is shorter than its diff:
```python
import functools

import jax
import jax.numpy as jnp
from jax import lax
from jax.experimental import pallas as pl
from jax.experimental.pallas import tpu as pltpu
from jax.sharding import PartitionSpec as P

LB = 128
KSEL = 3
HEADS = 12
HD = 64
PAIRS = HEADS // 2
LOG2E = 1.4426950408889634

F32 = jnp.float32
BF16 = jnp.bfloat16
MIB = 1024 * 1024

SMEM = pl.BlockSpec(memory_space=pltpu.SMEM)
VMEM = pl.BlockSpec(memory_space=pltpu.VMEM)
ANY = pl.BlockSpec(memory_space=pl.ANY)


def dot(a, b):
    return jnp.dot(a, b, preferred_element_type=F32)


def dot_last(a, b):
    return lax.dot_general(a, b, (((1,), (1,)), ((), ())), preferred_element_type=F32)


def pack_kernel(place_ref, cube_ref, optical_ref, near_ref, far_ref, unit_ref, wide_ref):
    chans, side, columns = cube_ref.shape
    nfreq = columns // side
    half = nfreq // 2
    mine = place_ref[0]
    wide_ref[...] = cube_ref[...].astype(F32).reshape(chans * side, columns)
    for r in range(side):
        turned = wide_ref[pl.ds(r, chans, stride=side), :].T.astype(BF16)
        at = slice(r * side, (r + 1) * side)
        for y in range(half):
            d = (y - mine) & (half - 1)
            low = turned[y * side : (y + 1) * side, :]
            high = turned[(half + y) * side : (half + y + 1) * side, :]
            near_ref[d, at, :] = jnp.where(mine < half, low, high)
            far_ref[d, at, :] = jnp.where(mine < half, high, low)
    optical = optical_ref[...].astype(F32)
    unit = (optical * lax.rsqrt(jnp.sum(optical * optical, axis=-1, keepdims=True) + 1e-06)).astype(BF16)
    unit_ref[...] = jnp.concatenate([unit[:, q * LB : (q + 1) * LB] for q in range(unit.shape[1] // LB)], axis=0)


def merge_kernel(near_ref, far_ref, *refs):
    pixels = near_ref.shape[1]
    unit_refs, out_refs = refs[:4], refs[4:]
    rows = unit_refs[0].shape[0]
    for d, out_ref in enumerate(out_refs, 1):
        out_ref[:pixels, :] = near_ref[d]
        out_ref[pixels : 2 * pixels, :] = far_ref[d]
        for n, unit_ref in enumerate(unit_refs):
            out_ref[2 * pixels + n * rows : 2 * pixels + (n + 1) * rows, :] = unit_ref[...]


def load_kernel(pos_hbm, w_in_hbm, wq_hbm, wk_hbm, wv_hbm, pos_ref, w_in_ref, wq_ref, wkt_ref, wv_ref, wk_ref, sems):
    copies = [
        pltpu.make_async_copy(source, target, sems.at[n])
        for n, (source, target) in enumerate(
            [(wk_hbm, wk_ref), (w_in_hbm, w_in_ref), (pos_hbm, pos_ref), (wq_hbm, wq_ref), (wv_hbm, wv_ref)]
        )
    ]
    for copy in copies:
        copy.start()
    copies[0].wait()
    wkt_ref[...] = wk_ref[...].T
    for copy in copies[1:]:
        copy.wait()


def project_kernel(
    place_ref, near_ref, far_ref, one_ref, two_ref, three_ref, gain_ref, pos_ref, w_in_ref, wq_ref, wkt_ref, wv_ref,
    tokens_ref, q_ref, kt_ref, v_ref, sum_ref,
):
    chans = pos_ref.shape[0]
    pixels, width = w_in_ref.shape
    half = chans // LB // 2

    mine = place_ref[0]
    same, other = mine & half, half - (mine & half)
    pieces, blocks = [], []
    for d, ref in enumerate((None, one_ref, two_ref, three_ref)):
        source = (mine - d) & (half - 1)
        pieces.append(near_ref.at[0] if d == 0 else ref.at[:pixels])
        blocks.append(same + source)
        pieces.append(far_ref.at[0] if d == 0 else ref.at[pixels : 2 * pixels])
        blocks.append(other + source)

    total = pieces[0][...].astype(F32)
    for piece in pieces[1:]:
        total += piece[...].astype(F32)
    centre = jnp.sum(total, axis=1, keepdims=True) * (1.0 / chans)
    total = jnp.zeros((pixels, LB), F32)
    for piece in pieces:
        gap = piece[...].astype(F32) - centre
        total += gap * gap
    inverse = lax.rsqrt(jnp.sum(total, axis=1, keepdims=True) * (1.0 / chans) + 1e-05)

    row = lax.broadcasted_iota(jnp.int32, (256, 256), 0) // HD
    col = lax.broadcasted_iota(jnp.int32, (256, 256), 1) // HD
    same_head = jnp.where(row == col, 1.0, 0.0).astype(BF16)

    per = 2
    token_sum = jnp.zeros((1, width), F32)
    for i in range(0, len(pieces), per):
        places = [pl.ds(pl.multiple_of(b * LB, LB), LB) for b in blocks[i : i + per]]
        unit = jnp.concatenate(
            [((piece[...].astype(F32) - centre) * inverse).astype(BF16) for piece in pieces[i : i + per]], axis=1
        )
        tokens = lax.dot_general(unit, w_in_ref[...], (((0,), (0,)), ((), ())), preferred_element_type=F32)
        tokens += jnp.concatenate([pos_ref[at, :] for at in places], axis=0).astype(F32)
        square_mean = jnp.mean(tokens * tokens, axis=-1, keepdims=True)
        normed = (tokens * lax.rsqrt(square_mean + 1e-06) * gain_ref[...]).astype(BF16)
        token_sum += jnp.sum(tokens, axis=0, keepdims=True)
        for n, at in enumerate(places):
            tokens_ref[at, :] = tokens[n * LB : (n + 1) * LB]
        for c in range(width // 256):
            part = slice(c * 256, (c + 1) * 256)
            q = dot(normed, wq_ref[:, part])
            squares = q * q
            high = squares.astype(BF16)
            low = (squares - high.astype(F32)).astype(BF16)
            length = dot(high, same_head) + dot(low, same_head)
            q = (q * lax.rsqrt(length + 1e-06)).astype(BF16)
            for n, at in enumerate(places):
                q_ref[at, part] = q[n * LB : (n + 1) * LB]
        kt = dot_last(wkt_ref[...], normed)
        kt = kt.reshape(HEADS, HD, per * LB)
        length = jnp.sum(kt * kt, axis=1, keepdims=True)
        kt = (kt * lax.rsqrt(length + 1e-06)).astype(BF16).reshape(width, per * LB)
        v = dot(normed, wv_ref[...]).astype(BF16)
        for n, at in enumerate(places):
            kt_ref[blocks[i + n]] = kt[:, n * LB : (n + 1) * LB]
            v_ref[at, :] = v[n * LB : (n + 1) * LB]
    sum_ref[...] = token_sum


def attend_kernel(
    pattern_ref, scale_ref, q_ref, kt_ref, v_ref, sum_ref, wo_hbm, wproj_hbm,
    heads_ref, proj_ref,
    wo_ref, wproj_ref, sems,
):
    chans, width = q_ref.shape
    nblocks = chans // LB
    copies = [
        pltpu.make_async_copy(wo_hbm, wo_ref, sems.at[0]),
        pltpu.make_async_copy(wproj_hbm, wproj_ref, sems.at[1]),
    ]
    for copy in copies:
        copy.start()

    lower = lax.broadcasted_iota(jnp.int32, (KSEL * LB, LB), 1) < HD
    ones = jnp.ones((KSEL * LB, LB), BF16)
    zeros = jnp.zeros((KSEL * LB, LB), BF16)
    sums = jnp.concatenate([jnp.where(lower, ones, zeros), jnp.where(lower, zeros, ones)], axis=0)
    blank = jnp.zeros((HD, KSEL * LB), BF16)

    def attend(b, heads_sum):
        at = pl.ds(pl.multiple_of(b * LB, LB), LB)
        chosen = [pattern_ref[b, j] for j in range(KSEL)]
        parts = []
        for p in range(PAIRS):
            part = slice(p * LB, (p + 1) * LB)
            kt = jnp.concatenate([kt_ref[c, part, :] for c in chosen], axis=1)
            keys = jnp.concatenate(
                [jnp.concatenate([kt[:HD], blank], axis=0), jnp.concatenate([blank, kt[HD:]], axis=0)], axis=1
            )
            scores = dot(q_ref[at, part], keys)
            half = KSEL * LB
            weights = jnp.concatenate(
                [
                    jnp.exp2(scores[:, :half] * (scale_ref[2 * p] * LOG2E)).astype(BF16),
                    jnp.exp2(scores[:, half:] * (scale_ref[2 * p + 1] * LOG2E)).astype(BF16),
                ],
                axis=1,
            )
            v = jnp.concatenate([v_ref[pl.ds(pl.multiple_of(c * LB, LB), LB), part] for c in chosen], axis=0)
            values = jnp.concatenate([jnp.where(lower, v, zeros), jnp.where(lower, zeros, v)], axis=0)
            both = dot(weights, jnp.concatenate([values, sums], axis=1))
            out = (both[:, :LB] / both[:, LB:]).astype(BF16)
            heads_ref[at, part] = out
            parts.append(jnp.sum(out.astype(F32), axis=0, keepdims=True))
        return heads_sum + jnp.concatenate(parts, axis=1)

    heads_sum = lax.fori_loop(0, nblocks, attend, jnp.zeros((1, width), F32))

    heads_mean = heads_sum * (1.0 / chans)
    first = heads_mean.astype(BF16)
    rest = heads_mean - first.astype(F32)
    second = rest.astype(BF16)
    third = (rest - second.astype(F32)).astype(BF16)
    rows = jnp.concatenate([first, second, third, jnp.zeros((13, width), BF16)], axis=0)
    for copy in copies:
        copy.wait()
    mixed = jnp.sum(dot(rows, wo_ref[...]), axis=0, keepdims=True)
    pooled = (sum_ref[...] * (1.0 / chans) + mixed).astype(BF16)
    pooled = jnp.broadcast_to(pooled, (16, width))
    proj_ref[...] = dot(pooled, wproj_ref[...])[:1]


def spread_kernel(place_ref, proj_ref, even_ref, odd_ref, mix_ref, first_ref, own_ref, second_ref):
    column_odd, row_odd = place_ref[0] & 1 != 0, place_ref[1] & 1 != 0
    before = jnp.where(column_odd, even_ref[...], odd_ref[...])
    after = jnp.where(column_odd, odd_ref[...], even_ref[...])
    down, own, up = (
        mix_ref[a, 0:1] * before + mix_ref[a, 1:2] * proj_ref[...] + mix_ref[a, 2:3] * after for a in range(3)
    )
    own_ref[...] = own
    first_ref[...] = jnp.where(row_odd, up, down)
    second_ref[...] = jnp.where(row_odd, down, up)


def loss_kernel(sizes, place_ref, scale_ref, target_ref, first_ref, own_ref, second_ref, *refs):
    nfreq, nsy, nsx, held = sizes
    optical_refs, (embed_ref, loss_ref) = refs[:nsx], refs[nsx:]
    mixed = first_ref[...] + own_ref[...] + second_ref[...]
    embed_ref[...] = mixed
    unit = (mixed * lax.rsqrt(jnp.sum(mixed * mixed) + 1e-06)).astype(BF16)
    quarters = mixed.shape[1] // LB
    unit = jnp.concatenate(
        [unit[:, q * LB : (q + 1) * LB] for q in range(quarters)] + [jnp.zeros((16 - quarters, LB), BF16)], axis=0
    )
    rows = optical_refs[0].shape[0]
    place = lax.broadcasted_iota(jnp.int32, (1, rows), 1)
    first = (place // held) % quarters == 0
    parts = []
    for ref in optical_refs:
        products = dot_last(unit, ref[...])
        logits = products[0:1]
        for q in range(1, quarters):
            logits = logits + pltpu.roll(products[q : q + 1], rows - q * held, 1)
        parts.append(logits)
    logits = jnp.concatenate(parts, axis=1) * scale_ref[0]
    place = lax.broadcasted_iota(jnp.int32, logits.shape, 1)
    logits = jnp.where(jnp.concatenate([first] * nsx, axis=1), logits, -jnp.inf)
    highest = jnp.max(logits, axis=1, keepdims=True)
    summed = jnp.sum(jnp.exp(logits - highest), axis=1, keepdims=True)

    half = nfreq // 2
    target = target_ref[0]
    k = target % held
    device = target // held
    sx = (place_ref[2] - device) & (nsx - 1)
    sy = (device // nsx) % nsy
    sy = (((place_ref[1] >> 1) - (sy >> 1)) & (nsy // 2 - 1)) * 2 + ((place_ref[1] ^ sy) & 1)
    f = device // (nsx * nsy)
    flipped = jnp.where((f ^ place_ref[0]) & half != 0, 1, 0)
    y = (place_ref[0] - f) & (half - 1)
    where = ((((sx * 2 + flipped) * half + y) * nsy + sy) * quarters) * held + k
    positive = jnp.sum(jnp.where(place == where, logits, 0.0), axis=1, keepdims=True)
    loss_ref[...] = jnp.log(summed) + highest - positive


def vmem(mib):
    return pltpu.CompilerParams(vmem_limit_bytes=mib * MIB)


def load(pos_embed, w_in, w_query, w_key, w_value):
    weights = (pos_embed, w_in, w_query, w_key, w_value)
    return pl.pallas_call(
        load_kernel,
        out_shape=tuple(jax.ShapeDtypeStruct(w.shape, BF16) for w in weights),
        in_specs=[ANY] * 5,
        out_specs=(VMEM,) * 5,
        scratch_shapes=[pltpu.VMEM(w_key.shape, BF16), pltpu.SemaphoreType.DMA((5,))],
        compiler_params=vmem(16),
        cost_estimate=pl.CostEstimate(flops=0, bytes_accessed=14_000_000, transcendentals=0),
    )(*weights)


def project(place, pieces, norm_gain, weights):
    chans, width = weights[0].shape
    return pl.pallas_call(
        project_kernel,
        out_shape=(
            jax.ShapeDtypeStruct((chans, width), F32),
            jax.ShapeDtypeStruct((chans, width), BF16),
            jax.ShapeDtypeStruct((chans // LB, width, LB), BF16),
            jax.ShapeDtypeStruct((chans, width), BF16),
            jax.ShapeDtypeStruct((1, width), F32),
        ),
        in_specs=[SMEM] + [VMEM] * (len(pieces) + 6),
        out_specs=(VMEM,) * 5,
        compiler_params=vmem(32),
        cost_estimate=pl.CostEstimate(flops=8_000_000_000, bytes_accessed=12_000_000, transcendentals=1_000_000),
    )(place, *pieces, norm_gain.reshape(1, width), *weights)


def attend(choose, attn_scale, queries, keys, values, token_sum, w_out, w_proj):
    chans, width = queries.shape
    return pl.pallas_call(
        attend_kernel,
        out_shape=(
            jax.ShapeDtypeStruct((chans, width), BF16),
            jax.ShapeDtypeStruct((1, w_proj.shape[1]), F32),
        ),
        in_specs=[SMEM, SMEM, VMEM, VMEM, VMEM, VMEM, ANY, ANY],
        out_specs=(VMEM, VMEM),
        scratch_shapes=[
            pltpu.VMEM(w_out.shape, BF16), pltpu.VMEM(w_proj.shape, BF16), pltpu.SemaphoreType.DMA((2,))
        ],
        compiler_params=vmem(40),
        cost_estimate=pl.CostEstimate(flops=8_000_000_000, bytes_accessed=8_000_000, transcendentals=5_000_000),
    )(choose, attn_scale, queries, keys, values, token_sum, w_out, w_proj)


def pairs(length, begin):
    return [pair for i in range(begin, length - 1, 2) for pair in ((i, i + 1), (i + 1, i))]


def column_pairs(begin, nfreq, nsx):
    def index(c):
        return c % nfreq * nsx + c // nfreq

    return [(index(a), index(b)) for a, b in pairs(nfreq * nsx, begin)]


def per_device(
    cube, pos_embed, w_in, norm_gain, w_query, w_key, w_value, w_out, attn_scale, w_proj, mix_weight, optical,
    logit_scale, pattern, match_ids,
):
    nfreq, nsy, nsx = (lax.axis_size(axis) for axis in ("freq", "sy", "sx"))
    half = nfreq // 2
    place = jnp.stack([lax.axis_index(axis) for axis in ("freq", "sy", "sx")]).astype(jnp.int32)
    local_chans, side = cube.shape[:2]
    pixels = side * side
    held, width = optical.shape
    rows = held * width // LB

    def steps_y(array, d):
        return lax.ppermute(array, "freq", [(i, i // half * half + (i + d) % half) for i in range(nfreq)])

    def other_half(array):
        return lax.ppermute(array, "freq", [(i, (i + half) % nfreq) for i in range(nfreq)])

    blocks = jax.ShapeDtypeStruct((half, pixels, local_chans), BF16)
    near, far, unit = pl.pallas_call(
        pack_kernel,
        out_shape=(blocks, blocks, jax.ShapeDtypeStruct((rows, LB), BF16)),
        in_specs=[SMEM, VMEM, VMEM],
        out_specs=(VMEM,) * 3,
        scratch_shapes=[pltpu.VMEM((local_chans * side, cube.shape[2]), F32)],
        compiler_params=vmem(8),
    )(place, cube, optical)
    far = other_half(far)
    far, *weights = lax.optimization_barrier((far, pos_embed, w_in, w_query, w_key, w_value))
    unit = jnp.concatenate([unit, lax.ppermute(unit, "sy", [(i, i ^ 1) for i in range(nsy)])], axis=0)
    units = [unit] + [lax.ppermute(unit, "sy", [(i, (i + 2 * d) % nsy) for i in range(nsy)]) for d in range(1, nsy // 2)]
    sent = pl.pallas_call(
        merge_kernel,
        out_shape=(jax.ShapeDtypeStruct((2 * pixels + nsy * rows, LB), BF16),) * (half - 1),
        in_specs=[VMEM] * (2 + len(units)),
        out_specs=(VMEM,) * (half - 1),
        compiler_params=vmem(8),
    )(near, far, *units)
    taken = [steps_y(array, d) for d, array in enumerate(sent, 1)]

    candidates = jnp.concatenate(units + [array[2 * pixels :] for array in taken], axis=0)
    others = other_half(candidates)
    tokens, queries, keys, values, token_sum = project(
        place, [near, far] + taken, norm_gain, load(*weights)
    )
    others, token_sum = lax.optimization_barrier((others, token_sum))
    candidates = jnp.concatenate([candidates, others], axis=0)
    candidates = [candidates] + [
        lax.ppermute(candidates, "sx", [(i, (i + d) % nsx) for i in range(nsx)]) for d in range(1, nsx)
    ]
    choose = pattern.reshape(pattern.shape[3], pattern.shape[4])
    heads_out, proj = attend(choose, attn_scale, queries, keys, values, token_sum, w_out, w_proj)
    proj, *candidates = lax.optimization_barrier((proj, *candidates))
    layer_out = (tokens + dot(heads_out, w_out)).astype(BF16)

    even = lax.ppermute(proj, ("freq", "sx"), column_pairs(0, nfreq, nsx))
    odd = lax.ppermute(proj, ("freq", "sx"), column_pairs(1, nfreq, nsx))
    line = jax.ShapeDtypeStruct((1, width), F32)
    first, own, second = pl.pallas_call(
        spread_kernel,
        out_shape=(line,) * 3,
        in_specs=[SMEM] + [VMEM] * 4,
        out_specs=(VMEM,) * 3,
        compiler_params=vmem(4),
    )(place, proj, even, odd, mix_weight)
    first = lax.ppermute(first, "sy", pairs(nsy, 0))
    second = lax.ppermute(second, "sy", pairs(nsy, 1))
    embed, loss = pl.pallas_call(
        functools.partial(loss_kernel, (nfreq, nsy, nsx, held)),
        out_shape=(line, jax.ShapeDtypeStruct((1, 1), F32)),
        in_specs=[SMEM] * 3 + [VMEM] * (3 + nsx),
        out_specs=(VMEM, VMEM),
        compiler_params=vmem(8),
    )(place, logit_scale, match_ids.reshape(1), first, own, second, *candidates)
    return (
        layer_out.reshape((1, 1, 1) + layer_out.shape),
        embed.reshape(1, 1, 1, width),
        loss.reshape(1, 1, 1),
    )


def solution(mesh):
    in_specs = (
        P("freq", "sy", "sx"), P(), P(), P(), P(), P(), P(), P(), P(), P(), P(),
        P(("freq", "sy", "sx"), None), P(), P("sy", "sx", "freq", None, None), P("sy", "sx", "freq"),
    )
    out_specs = (
        P("sy", "sx", "freq", None, None),
        P("sy", "sx", "freq", None),
        P("sy", "sx", "freq"),
    )
    return jax.shard_map(per_device, mesh=mesh, in_specs=in_specs, out_specs=out_specs, check_vma=False)
```

time: 571 us -> 86.9 us (0.15)
  waiting for transfers between devices: 411 us -> 7.02 us
  matrix products: 52.3 us -> 1.39 us
  other arithmetic: 32.2 us -> 1.69 us
  Pallas kernels: 0 us -> 23.7 us
  between operations: 20.2 us -> 2.13 us
  local copies, waits for them, and re-layouts: 21.5 us -> 8.32 us
  starting transfers between devices: 31.3 us -> 42.3 us
    all_gather x1 -> x0, waiting for transfers between devices: 387 us -> none  [per_device(): lax.all_gather(optical_unit, ('freq', 'sy', 'sx'), axis=0, tiled=True)]
    dot_general x9 -> x1, matrix products: 52.3 us -> 1.39 us  [dot(): return jnp.dot(a, b, preferred_element_type=F32)]
    pallas_call x0 -> x7, Pallas kernels: none -> 23.7 us  [the longest x1 9.59 us: project(): pl.pallas_call(project_kernel, out_shape=(jax.ShapeDtypeStruct((chans, wi...]
    ppermute x6 -> x16, starting transfers between devices: 20.5 us -> 42.3 us  [the longest x1 9.51 us: per_device(): odd = lax.ppermute(proj, ('freq', 'sx'), column_pairs(1, nfreq, nsx))]
    sub x1 -> x0, other arithmetic: 15.6 us -> none  [attention_layer(): weights = jnp.exp(scores - highest)]
    all_to_all x1 -> x0, starting transfers between devices: 10.8 us -> none  [per_device(): lax.all_to_all(planes, 'freq', split_axis=0, concat_axis=1, tiled=True)[0]]
    all_to_all x1 -> x0, waiting for transfers between devices: 10.4 us -> none  [per_device(): lax.all_to_all(planes, 'freq', split_axis=0, concat_axis=1, tiled=True)[0]]
    unnamed x2 -> x0, other arithmetic: 7.51 us -> none
  transfers between devices with their start and end apart: 8 -> 16, of which waited for: 6 -> 3; matrix products, arithmetic and copies ran while one was open for 17% -> 5% of each run, Pallas kernels for 0% -> 23%
where the time goes in v1:
time: 86.9 us; the launch traced here: 86.5 us
  starting transfers between devices  42.3 us (49%)
  Pallas kernels  23.7 us (27%)
  local copies, waits for them, and re-layouts  8.32 us (10%)
  waiting for transfers between devices  7.02 us (8%)
  between operations  2.13 us (2%)
  other arithmetic  1.69 us (2%)
  matrix products  1.39 us (2%)
    pallas_call x1, Pallas kernels, project(): pl.pallas_call(project_kernel, out_shape=(jax.ShapeDtypeStruct((chans, wi...  9.59 us
    ppermute x1, starting transfers between devices, per_device(): odd = lax.ppermute(proj, ('freq', 'sx'), column_pairs(1, nfreq, nsx))  9.51 us
    pallas_call x1, Pallas kernels, attend(): pl.pallas_call(attend_kernel, out_shape=(jax.ShapeDtypeStruct((chans, wid...  9.24 us
    ppermute x1, starting transfers between devices, per_device(): first = lax.ppermute(first, 'sy', pairs(nsy, 0))  7.76 us
    ppermute x2, starting transfers between devices, other_half(): lax.ppermute(array, 'freq', [(i, (i + half) % nfreq) for i in range(nfreq)])  7.45 us
    unnamed x30, local copies, waits for them, and re-layouts  6.86 us
    ppermute x3, waiting for transfers between devices, per_device(): lax.ppermute(unit, 'sy', [(i, (i + 2 * d) % nsy) for i in range(nsy)])  6.69 us
    ppermute x3, starting transfers between devices, steps_y(): lax.ppermute(array, 'freq', [(i, i // half * half + (i + d) % half) for i...  5.14 us
  transfers between devices with their start and end apart: 16, of which 3 were waited for; matrix products, arithmetic and copies ran while one was open for 5% of the time, Pallas kernels for 23%

profile of v1, /device:TPU:3, one launch (start us, length us, event | category | flops | bytes accessed | tf_op | source)
XLA Modules:
  0.0 86.5 jit_solution(6042353191277560294)
XLA Ops:
  0.7 1.1 %copy-done.4 = bf16[128,16,128]{2,1,0:T(8,128)(2,1)S(1)} copy-done((bf16[128,16,128]{2,1,0:T(8,128)(2,1)S(1)}, bf16[128,16,128]{2,1,0:T(8,128)(2,1)}, u32[]{:S(2)}) %copy-start.4) | copy-done | bytes 524312
  1.8 0.7 copy-done.7
  2.5 1.0 %shard_map.166 = (bf16[4,256,128]{2,1,0:T(8,128)(2,1)S(1)}, bf16[4,256,128]{2,1,0:T(8,128)(2,1)S(1)}, bf16[16,128]{1,0:T(8,128)(2,1)S(1)}) custom-call(s32[3]{0:T(128)S(1)} %pad_add_fusion.place_ref, bf16[128,16,128]{2,1,0:T(8,128)(2,1)S(1)} %copy-done.4, bf16[4,512]{1,0:T(4,128)(2,1)S(1)} %copy-done.7), custom_call_target="tpu_custom_call" | custom-call | tf_op jit(solution)/shard_map/pallas_call | solution.py:346
  3.5 0.8 collective-permute-start.1
  4.3 6.9 %collective-permute-start = (bf16[4,256,128]{2,1,0:T(8,128)(2,1)S(1)}, bf16[4,256,128]{2,1,0:T(8,128)(2,1)S(1)}, u32[]{:S(2)}, u32[]{:S(2)}) collective-permute-start(bf16[4,256,128]{2,1,0:T(8,128)(2,1)S(1)} %get-tuple-element.40), channel_id=1, source_target_pairs={{0,128},{32,160},{64,192},{96,224},{128,0},{160,32},{192,64},{224,... | collective-permute-start | bytes 786440 | tf_op jit(solution)/shard_map/ppermute | solution.py:343
  11.2 0.8 collective-permute-start.2
  12.1 0.7 reshape.24.gain_ref
  12.8 0.8 copy.19
  14.8 1.3 %collective-permute-start.3 = (bf16[32,128]{1,0:T(8,128)(2,1)S(1)}, bf16[32,128]{1,0:T(8,128)(2,1)S(1)}, u32[]{:S(2)}, u32[]{:S(2)}) collective-permute-start(bf16[32,128]{1,0:T(8,128)(2,1)S(1)} %get-tuple-element.89.refs_0_), channel_id=1, source_target_pairs={{0,16},{4,20},{8,24},{12,28},{16,0},{20,4},{24,8},{28,12},{1,17},{... | collective-permute-start | bytes 24584 | tf_op jit(solution)/shard_map/ppermute | solution.py:357
  16.1 1.6 %collective-permute-start.4 = (bf16[32,128]{1,0:T(8,128)(2,1)S(1)}, bf16[32,128]{1,0:T(8,128)(2,1)S(1)}, u32[]{:S(2)}, u32[]{:S(2)}) collective-permute-start(bf16[32,128]{1,0:T(8,128)(2,1)S(1)} %get-tuple-element.89.refs_0_), channel_id=1, source_target_pairs={{0,24},{4,28},{8,0},{12,4},{16,8},{20,12},{24,16},{28,20},{1,25},{... | collective-permute-start | bytes 24584 | tf_op jit(solution)/shard_map/ppermute | solution.py:357
  17.7 5.3 %collective-permute-done.2.refs_1_ = bf16[32,128]{1,0:T(8,128)(2,1)S(1)} collective-permute-done((bf16[32,128]{1,0:T(8,128)(2,1)S(1)}, bf16[32,128]{1,0:T(8,128)(2,1)S(1)}, u32[]{:S(2)}, u32[]{:S(2)}) %collective-permute-start.2) | collective-permute-done | bytes 8224 | tf_op jit(solution)/shard_map/ppermute | solution.py:357
  23.0 1.4 %collective-permute-done.4.refs_3_ = bf16[32,128]{1,0:T(8,128)(2,1)S(1)} collective-permute-done((bf16[32,128]{1,0:T(8,128)(2,1)S(1)}, bf16[32,128]{1,0:T(8,128)(2,1)S(1)}, u32[]{:S(2)}, u32[]{:S(2)}) %collective-permute-start.4) | collective-permute-done | bytes 8224 | tf_op jit(solution)/shard_map/ppermute | solution.py:357
  24.5 1.4 %collective-permute-start.5 = (bf16[640,128]{1,0:T(8,128)(2,1)S(1)}, bf16[640,128]{1,0:T(8,128)(2,1)S(1)}, u32[]{:S(2)}, u32[]{:S(2)}) collective-permute-start(bf16[640,128]{1,0:T(8,128)(2,1)S(1)} %get-tuple-element.43), channel_id=1, source_target_pairs={{0,32},{32,64},{64,96},{96,0},{128,160},{160,192},{192,224},{224,1... | collective-permute-start | bytes 491528 | tf_op jit(solution)/shard_map/ppermute | solution.py:340
  25.9 2.7 %collective-permute-start.6 = (bf16[640,128]{1,0:T(8,128)(2,1)S(1)}, bf16[640,128]{1,0:T(8,128)(2,1)S(1)}, u32[]{:S(2)}, u32[]{:S(2)}) collective-permute-start(bf16[640,128]{1,0:T(8,128)(2,1)S(1)} %get-tuple-element.44), channel_id=1, source_target_pairs={{0,64},{32,96},{64,0},{96,32},{128,192},{160,224},{192,128},{224,1... | collective-permute-start | bytes 491528 | tf_op jit(solution)/shard_map/ppermute | solution.py:340
  28.6 1.1 %collective-permute-start.7 = (bf16[640,128]{1,0:T(8,128)(2,1)S(1)}, bf16[640,128]{1,0:T(8,128)(2,1)S(1)}, u32[]{:S(2)}, u32[]{:S(2)}) collective-permute-start(bf16[640,128]{1,0:T(8,128)(2,1)S(1)} %get-tuple-element.45), channel_id=1, source_target_pairs={{0,96},{32,0},{64,32},{96,64},{128,224},{160,128},{192,160},{224,1... | collective-permute-start | bytes 491528 | tf_op jit(solution)/shard_map/ppermute | solution.py:340
  29.6 1.4 %copy-done = bf16[1024,768]{1,0:T(8,128)(2,1)S(1)} copy-done((bf16[1024,768]{1,0:T(8,128)(2,1)S(1)}, bf16[1024,768]{1,0:T(8,128)(2,1)}, u32[]{:S(2)}) %copy-start) | copy-done | bytes 1572888
  31.0 1.3 %copy-done.2 = bf16[768,768]{1,0:T(8,128)(2,1)S(1)} copy-done((bf16[768,768]{1,0:T(8,128)(2,1)S(1)}, bf16[768,768]{1,0:T(8,128)(2,1)}, u32[]{:S(2)}) %copy-start.2) | copy-done | bytes 1179672
  32.3 1.3 %copy-done.3 = bf16[768,768]{1,0:T(8,128)(2,1)S(1)} copy-done((bf16[768,768]{1,0:T(8,128)(2,1)S(1)}, bf16[768,768]{1,0:T(8,128)(2,1)}, u32[]{:S(2)}) %copy-start.3) | copy-done | bytes 1179672
  33.6 1.0 %copy-done.5 = bf16[256,768]{1,0:T(8,128)(2,1)S(1)} copy-done((bf16[256,768]{1,0:T(8,128)(2,1)S(1)}, bf16[256,768]{1,0:T(8,128)(2,1)}, u32[]{:S(2)}) %copy-start.5) | copy-done | bytes 393240
  34.6 1.4 %shard_map.168 = (bf16[1024,768]{1,0:T(8,128)(2,1)S(1)}, bf16[256,768]{1,0:T(8,128)(2,1)S(1)}, bf16[768,768]{1,0:T(8,128)(2,1)S(1)}, bf16[768,768]{1,0:T(8,128)(2,1)S(1)}, bf16[768,768]{1,0:T(8,128)(2,1)S(1)}) custom-call(bf16[1024,768]{1,0:T(8,128)(2,1)S(1)} %copy-done, bf16[256,768]{1,0:T(8,128)(2,1)S(1)} %copy-done.5, bf16[768,768]{1,0:T(8,128)(2,1)S(1)} %copy-done.1, ...), custom_call_target="tpu_custom_call" | custom-call | bytes 14000000 | tf_op jit(solution)/shard_map/pallas_call | solution.py:269
  36.6 9.6 %shard_map.169 = (f32[1024,768]{1,0:T(8,128)S(1)}, bf16[1024,768]{1,0:T(8,128)(2,1)S(1)}, bf16[8,768,128]{2,1,0:T(8,128)(2,1)S(1)}, bf16[1024,768]{1,0:T(8,128)(2,1)S(1)}, f32[1,768]{1,0:T(1,128)S(1)}) custom-call(s32[3]{0:T(128)S(1)} %pad_add_fusion.place_ref, bf16[4,256,128]{2,1,0:T(8,128)(2,1)S(1)} %get-tuple-element.39.near_ref, ...), custom_call_target="tpu_custom_call" | custom-call | flops 8000000000 | bytes 12000000 | tf_op jit(solution)/shard_map/pallas_call | solution.py:282
  46.3 1.9 %collective-permute-start.10 = (bf16[1024,128]{1,0:T(8,128)(2,1)S(1)}, bf16[1024,128]{1,0:T(8,128)(2,1)S(1)}, u32[]{:S(2)}, u32[]{:S(2)}) collective-permute-start(bf16[1024,128]{1,0:T(8,128)(2,1)S(1)} %constant_dynamic-update-slice_fusion.10.refs_0_), channel_id=1, source_target_pairs={{0,2},{1,3},{2,0},{3,1},{4,6},{5,7},{6,4},{7,5},{8,10},{9,11},{10,... | collective-permute-start | bytes 786440 | tf_op jit(solution)/shard_map/ppermute | solution.py:375
  48.2 1.2 %collective-permute-start.11 = (bf16[1024,128]{1,0:T(8,128)(2,1)S(1)}, bf16[1024,128]{1,0:T(8,128)(2,1)S(1)}, u32[]{:S(2)}, u32[]{:S(2)}) collective-permute-start(bf16[1024,128]{1,0:T(8,128)(2,1)S(1)} %constant_dynamic-update-slice_fusion.10.refs_0_), channel_id=1, source_target_pairs={{0,3},{1,0},{2,1},{3,2},{4,7},{5,4},{6,5},{7,6},{8,11},{9,8},{10,9... | collective-permute-start | bytes 786440 | tf_op jit(solution)/shard_map/ppermute | solution.py:375
  49.7 9.2 %shard_map.170 = (bf16[1024,768]{1,0:T(8,128)(2,1)S(1)}, f32[1,512]{1,0:T(1,128)S(1)}) custom-call(s32[8,3]{1,0:T(8,128)S(1)} %bitcast.12, f32[12]{0:T(128)S(1)} %copy-done.10, bf16[1024,768]{1,0:T(8,128)(2,1)S(1)} %get-tuple-element.57.q_ref, bf16[8,768,128]{2,1,0:T(8,128)(2,1)S(1)} %get-tuple-element.58.kt_ref, ...), custom_call_target="tpu_custom_call" | custom-call | flops 8000000000 | bytes 8000000 | tf_op jit(solution)/shard_map/pallas_call | solution.py:300
  58.9 0.6 collective-permute-start.12
  59.5 9.5 %collective-permute-start.13 = (f32[1,512]{1,0:T(1,128)S(1)}, f32[1,512]{1,0:T(1,128)S(1)}, u32[]{:S(2)}, u32[]{:S(2)}) collective-permute-start(f32[1,512]{1,0:T(1,128)S(1)} %get-tuple-element.65.proj_ref), channel_id=1, source_target_pairs={{32,64},{64,32},{96,128},{128,96},{160,192},{192,160},{224,1},{1,2... | collective-permute-start | bytes 6152 | tf_op jit(solution)/shard_map/ppermute | solution.py:383
  69.1 1.4 %fusion.1 = f32[1024,768]{1,0:T(8,128)S(1)} fusion(bf16[1024,768]{1,0:T(8,128)(2,1)S(1)} %get-tuple-element.62, bf16[768,768]{1,0:T(8,128)(2,1)S(1)} %copy-done.8), kind=kOutput, calls=%fused_computation.22 | convolution fusion | flops 1207959552 | bytes 5898240 | tf_op jit(solution)/shard_map/dot_general | solution.py:27
  70.8 0.6 shard_map.171
  71.3 7.8 %collective-permute-start.14 = (f32[1,512]{1,0:T(1,128)S(1)}, f32[1,512]{1,0:T(1,128)S(1)}, u32[]{:S(2)}, u32[]{:S(2)}) collective-permute-start(f32[1,512]{1,0:T(1,128)S(1)} %get-tuple-element.66), channel_id=1, source_target_pairs={{0,4},{4,0},{8,12},{12,8},{16,20},{20,16},{24,28},{28,24},{1,5},{5... | collective-permute-start | bytes 6152 | tf_op jit(solution)/shard_map/ppermute | solution.py:392
  79.1 3.9 %collective-permute-start.15 = (f32[1,512]{1,0:T(1,128)S(1)}, f32[1,512]{1,0:T(1,128)S(1)}, u32[]{:S(2)}, u32[]{:S(2)}) collective-permute-start(f32[1,512]{1,0:T(1,128)S(1)} %get-tuple-element.68), channel_id=1, source_target_pairs={{4,8},{8,4},{12,16},{16,12},{20,24},{24,20},{5,9},{9,5},{13,17},{1... | collective-permute-start | bytes 6152 | tf_op jit(solution)/shard_map/ppermute | solution.py:393
  83.1 1.6 %fusion = bf16[1,1,1,1024,768]{4,3,2,1,0:T(8,128)(2,1)} fusion(f32[1024,768]{1,0:T(8,128)S(1)} %get-tuple-element.56, f32[1024,768]{1,0:T(8,128)S(1)} %fusion.1), kind=kLoop, calls=%fused_computation.1 | loop fusion | flops 1572864 | bytes 7864320 | tf_op jit(solution)/shard_map/reshape | solution.py:402
  84.7 1.9 %shard_map.172 = (f32[1,512]{1,0:T(1,128)}, f32[1,1]{1,0:T(1,128)}) custom-call(s32[3]{0:T(128)S(1)} %pad_add_fusion.place_ref, f32[1]{0:T(128)S(6)} %copy.36.scale_ref, s32[1]{0:T(128)} %bitcast.11.target_ref, f32[1,512]{1,0:T(1,128)S(1)} %collective-permute-done.14.first_ref, f32[1,512]{1,0:T(1,128)S(1)} %get-tuple-element.67.own_ref, ...), custom_call_target="tpu_custom_call" | custom-call | tf_op jit(solution)/shard_map/pallas_call | solution.py:394
  (43 shorter events, 1.4 us)
Async XLA Ops:
  0.6 29.0 %copy-start.1 = (bf16[768,768]{1,0:T(8,128)(2,1)S(1)}, bf16[768,768]{1,0:T(8,128)(2,1)}, u32[]{:S(2)}) copy-start(bf16[768,768]{1,0:T(8,128)(2,1)} %wq_hbm) | copy-start | bytes 3538948
  0.7 1.1 %copy-start.4 = (bf16[128,16,128]{2,1,0:T(8,128)(2,1)S(1)}, bf16[128,16,128]{2,1,0:T(8,128)(2,1)}, u32[]{:S(2)}) copy-start(bf16[128,16,128]{2,1,0:T(8,128)(2,1)} %cube_ref.1) | copy-start | bytes 1572868
  1.8 0.7 copy-start.7
  3.5 7.7 %collective-permute-start.1 = (bf16[16,128]{1,0:T(8,128)(2,1)S(1)}, bf16[16,128]{1,0:T(8,128)(2,1)S(1)}, u32[]{:S(2)}, u32[]{:S(2)}) collective-permute-start(bf16[16,128]{1,0:T(8,128)(2,1)S(1)} %get-tuple-element.42), channel_id=1, source_target_pairs={{0,4},{4,0},{8,12},{12,8},{16,20},{20,16},{24,28},{28,24},{1,5},{5... | collective-permute-start | bytes 12296 | tf_op jit(solution)/shard_map/ppermute | solution.py:356
  4.3 18.7 %collective-permute-start = (bf16[4,256,128]{2,1,0:T(8,128)(2,1)S(1)}, bf16[4,256,128]{2,1,0:T(8,128)(2,1)S(1)}, u32[]{:S(2)}, u32[]{:S(2)}) collective-permute-start(bf16[4,256,128]{2,1,0:T(8,128)(2,1)S(1)} %get-tuple-element.40), channel_id=1, source_target_pairs={{0,128},{32,160},{64,192},{96,224},{128,0},{160,32},{192,64},{224,... | collective-permute-start | bytes 786440 | tf_op jit(solution)/shard_map/ppermute | solution.py:343
  11.2 11.8 %collective-permute-start.2 = (bf16[32,128]{1,0:T(8,128)(2,1)S(1)}, bf16[32,128]{1,0:T(8,128)(2,1)S(1)}, u32[]{:S(2)}, u32[]{:S(2)}) collective-permute-start(bf16[32,128]{1,0:T(8,128)(2,1)S(1)} %get-tuple-element.89.refs_0_), channel_id=1, source_target_pairs={{0,8},{4,12},{8,16},{12,20},{16,24},{20,28},{24,0},{28,4},{1,9},{5... | collective-permute-start | bytes 24584 | tf_op jit(solution)/shard_map/ppermute | solution.py:357
  14.8 8.2 %collective-permute-start.3 = (bf16[32,128]{1,0:T(8,128)(2,1)S(1)}, bf16[32,128]{1,0:T(8,128)(2,1)S(1)}, u32[]{:S(2)}, u32[]{:S(2)}) collective-permute-start(bf16[32,128]{1,0:T(8,128)(2,1)S(1)} %get-tuple-element.89.refs_0_), channel_id=1, source_target_pairs={{0,16},{4,20},{8,24},{12,28},{16,0},{20,4},{24,8},{28,12},{1,17},{... | collective-permute-start | bytes 24584 | tf_op jit(solution)/shard_map/ppermute | solution.py:357
  16.1 8.3 %collective-permute-start.4 = (bf16[32,128]{1,0:T(8,128)(2,1)S(1)}, bf16[32,128]{1,0:T(8,128)(2,1)S(1)}, u32[]{:S(2)}, u32[]{:S(2)}) collective-permute-start(bf16[32,128]{1,0:T(8,128)(2,1)S(1)} %get-tuple-element.89.refs_0_), channel_id=1, source_target_pairs={{0,24},{4,28},{8,0},{12,4},{16,8},{20,12},{24,16},{28,20},{1,25},{... | collective-permute-start | bytes 24584 | tf_op jit(solution)/shard_map/ppermute | solution.py:357
  24.5 11.5 %collective-permute-start.5 = (bf16[640,128]{1,0:T(8,128)(2,1)S(1)}, bf16[640,128]{1,0:T(8,128)(2,1)S(1)}, u32[]{:S(2)}, u32[]{:S(2)}) collective-permute-start(bf16[640,128]{1,0:T(8,128)(2,1)S(1)} %get-tuple-element.43), channel_id=1, source_target_pairs={{0,32},{32,64},{64,96},{96,0},{128,160},{160,192},{192,224},{224,1... | collective-permute-start | bytes 491528 | tf_op jit(solution)/shard_map/ppermute | solution.py:340
  25.9 10.2 %collective-permute-start.6 = (bf16[640,128]{1,0:T(8,128)(2,1)S(1)}, bf16[640,128]{1,0:T(8,128)(2,1)S(1)}, u32[]{:S(2)}, u32[]{:S(2)}) collective-permute-start(bf16[640,128]{1,0:T(8,128)(2,1)S(1)} %get-tuple-element.44), channel_id=1, source_target_pairs={{0,64},{32,96},{64,0},{96,32},{128,192},{160,224},{192,128},{224,1... | collective-permute-start | bytes 491528 | tf_op jit(solution)/shard_map/ppermute | solution.py:340
  28.6 7.5 %collective-permute-start.7 = (bf16[640,128]{1,0:T(8,128)(2,1)S(1)}, bf16[640,128]{1,0:T(8,128)(2,1)S(1)}, u32[]{:S(2)}, u32[]{:S(2)}) collective-permute-start(bf16[640,128]{1,0:T(8,128)(2,1)S(1)} %get-tuple-element.45), channel_id=1, source_target_pairs={{0,96},{32,0},{64,32},{96,64},{128,224},{160,128},{192,160},{224,1... | collective-permute-start | bytes 491528 | tf_op jit(solution)/shard_map/ppermute | solution.py:340
  29.6 1.4 %copy-start = (bf16[1024,768]{1,0:T(8,128)(2,1)S(1)}, bf16[1024,768]{1,0:T(8,128)(2,1)}, u32[]{:S(2)}) copy-start(bf16[1024,768]{1,0:T(8,128)(2,1)} %pos_hbm) | copy-start | bytes 4718596
  31.0 1.3 %copy-start.2 = (bf16[768,768]{1,0:T(8,128)(2,1)S(1)}, bf16[768,768]{1,0:T(8,128)(2,1)}, u32[]{:S(2)}) copy-start(bf16[768,768]{1,0:T(8,128)(2,1)} %wk_hbm) | copy-start | bytes 3538948
  32.3 1.3 %copy-start.3 = (bf16[768,768]{1,0:T(8,128)(2,1)S(1)}, bf16[768,768]{1,0:T(8,128)(2,1)}, u32[]{:S(2)}) copy-start(bf16[768,768]{1,0:T(8,128)(2,1)} %wv_hbm) | copy-start | bytes 3538948
  33.6 1.0 %copy-start.5 = (bf16[256,768]{1,0:T(8,128)(2,1)S(1)}, bf16[256,768]{1,0:T(8,128)(2,1)}, u32[]{:S(2)}) copy-start(bf16[256,768]{1,0:T(8,128)(2,1)} %w_in_hbm) | copy-start | bytes 1179652
  36.1 10.1 %collective-permute-start.8 = (bf16[512,128]{1,0:T(8,128)(2,1)S(1)}, bf16[512,128]{1,0:T(8,128)(2,1)S(1)}, u32[]{:S(2)}, u32[]{:S(2)}) collective-permute-start(bf16[512,128]{1,0:T(8,128)(2,1)S(1)} %get-tuple-element.76), channel_id=1, source_target_pairs={{0,128},{32,160},{64,192},{96,224},{128,0},{160,32},{192,64},{224,... | collective-permute-start | bytes 393224 | tf_op jit(solution)/shard_map/ppermute | solution.py:343
  36.6 13.0 %copy-start.8 = (bf16[768,768]{1,0:T(8,128)(2,1)S(1)}, bf16[768,768]{1,0:T(8,128)(2,1)}, u32[]{:S(2)}) copy-start(bf16[768,768]{1,0:T(8,128)(2,1)} %wo_hbm.1) | copy-start | bytes 3538948
  36.6 13.0 %copy-start.9 = (bf16[768,512]{1,0:T(8,128)(2,1)S(1)}, bf16[768,512]{1,0:T(8,128)(2,1)}, u32[]{:S(2)}) copy-start(bf16[768,512]{1,0:T(8,128)(2,1)} %wproj_hbm.1) | copy-start | bytes 2359300
  36.6 13.0 %copy-start.10 = (f32[12]{0:T(128)S(1)}, f32[12]{0:T(128)}, u32[]{:S(2)}) copy-start(f32[12]{0:T(128)} %scale_ref.2) | copy-start | bytes 148
  46.3 12.7 %collective-permute-start.10 = (bf16[1024,128]{1,0:T(8,128)(2,1)S(1)}, bf16[1024,128]{1,0:T(8,128)(2,1)S(1)}, u32[]{:S(2)}, u32[]{:S(2)}) collective-permute-start(bf16[1024,128]{1,0:T(8,128)(2,1)S(1)} %constant_dynamic-update-slice_fusion.10.refs_0_), channel_id=1, source_target_pairs={{0,2},{1,3},{2,0},{3,1},{4,6},{5,7},{6,4},{7,5},{8,10},{9,11},{10,... | collective-permute-start | bytes 786440 | tf_op jit(solution)/shard_map/ppermute | solution.py:375
  48.2 10.7 %collective-permute-start.11 = (bf16[1024,128]{1,0:T(8,128)(2,1)S(1)}, bf16[1024,128]{1,0:T(8,128)(2,1)S(1)}, u32[]{:S(2)}, u32[]{:S(2)}) collective-permute-start(bf16[1024,128]{1,0:T(8,128)(2,1)S(1)} %constant_dynamic-update-slice_fusion.10.refs_0_), channel_id=1, source_target_pairs={{0,3},{1,0},{2,1},{3,2},{4,7},{5,4},{6,5},{7,6},{8,11},{9,8},{10,9... | collective-permute-start | bytes 786440 | tf_op jit(solution)/shard_map/ppermute | solution.py:375
  49.3 9.6 %collective-permute-start.9 = (bf16[1024,128]{1,0:T(8,128)(2,1)S(1)}, bf16[1024,128]{1,0:T(8,128)(2,1)S(1)}, u32[]{:S(2)}, u32[]{:S(2)}) collective-permute-start(bf16[1024,128]{1,0:T(8,128)(2,1)S(1)} %constant_dynamic-update-slice_fusion.10.refs_0_), channel_id=1, source_target_pairs={{0,1},{1,2},{2,3},{3,0},{4,5},{5,6},{6,7},{7,4},{8,9},{9,10},{10,1... | collective-permute-start | bytes 786440 | tf_op jit(solution)/shard_map/ppermute | solution.py:375
  58.9 11.5 %collective-permute-start.12 = (f32[1,512]{1,0:T(1,128)S(1)}, f32[1,512]{1,0:T(1,128)S(1)}, u32[]{:S(2)}, u32[]{:S(2)}) collective-permute-start(f32[1,512]{1,0:T(1,128)S(1)} %get-tuple-element.65.proj_ref), channel_id=1, source_target_pairs={{0,32},{32,0},{64,96},{96,64},{128,160},{160,128},{192,224},{224,1... | collective-permute-start | bytes 6152 | tf_op jit(solution)/shard_map/ppermute | solution.py:382
  59.5 11.2 %collective-permute-start.13 = (f32[1,512]{1,0:T(1,128)S(1)}, f32[1,512]{1,0:T(1,128)S(1)}, u32[]{:S(2)}, u32[]{:S(2)}) collective-permute-start(f32[1,512]{1,0:T(1,128)S(1)} %get-tuple-element.65.proj_ref), channel_id=1, source_target_pairs={{32,64},{64,32},{96,128},{128,96},{160,192},{192,160},{224,1},{1,2... | collective-permute-start | bytes 6152 | tf_op jit(solution)/shard_map/ppermute | solution.py:383
  69.1 1.7 %copy-start.6 = (f32[3,3,512]{2,1,0:T(4,128)S(1)}, f32[3,3,512]{2,1,0:T(4,128)}, u32[]{:S(2)}) copy-start(f32[3,3,512]{2,1,0:T(4,128)} %mix_ref.1) | copy-start | bytes 55300
  71.3 13.3 %collective-permute-start.14 = (f32[1,512]{1,0:T(1,128)S(1)}, f32[1,512]{1,0:T(1,128)S(1)}, u32[]{:S(2)}, u32[]{:S(2)}) collective-permute-start(f32[1,512]{1,0:T(1,128)S(1)} %get-tuple-element.66), channel_id=1, source_target_pairs={{0,4},{4,0},{8,12},{12,8},{16,20},{20,16},{24,28},{28,24},{1,5},{5... | collective-permute-start | bytes 6152 | tf_op jit(solution)/shard_map/ppermute | solution.py:392
  79.1 5.6 %collective-permute-start.15 = (f32[1,512]{1,0:T(1,128)S(1)}, f32[1,512]{1,0:T(1,128)S(1)}, u32[]{:S(2)}, u32[]{:S(2)}) collective-permute-start(f32[1,512]{1,0:T(1,128)S(1)} %get-tuple-element.68), channel_id=1, source_target_pairs={{4,8},{8,4},{12,16},{16,12},{20,24},{24,20},{5,9},{9,5},{13,17},{1... | collective-permute-start | bytes 6152 | tf_op jit(solution)/shard_map/ppermute | solution.py:393

commit v2 on v1

--- a/solution.py
+++ b/solution.py
@@ -53,28 +53,28 @@
 
 def merge_kernel(near_ref, far_ref, *refs):
     pixels = near_ref.shape[1]
-    unit_refs, out_refs = refs[:4], refs[4:]
-    rows = unit_refs[0].shape[0]
+    unit_refs, out_refs = refs[: -(near_ref.shape[0] - 1)], refs[-(near_ref.shape[0] - 1) :]
     for d, out_ref in enumerate(out_refs, 1):
         out_ref[:pixels, :] = near_ref[d]
         out_ref[pixels : 2 * pixels, :] = far_ref[d]
-        for n, unit_ref in enumerate(unit_refs):
-            out_ref[2 * pixels + n * rows : 2 * pixels + (n + 1) * rows, :] = unit_ref[...]
-
-
-def load_kernel(pos_hbm, w_in_hbm, wq_hbm, wk_hbm, wv_hbm, pos_ref, w_in_ref, wq_ref, wkt_ref, wv_ref, wk_ref, sems):
-    copies = [
-        pltpu.make_async_copy(source, target, sems.at[n])
-        for n, (source, target) in enumerate(
-            [(wk_hbm, wk_ref), (w_in_hbm, w_in_ref), (pos_hbm, pos_ref), (wq_hbm, wq_ref), (wv_hbm, wv_ref)]
-        )
-    ]
+        row = 2 * pixels
+        for unit_ref in unit_refs:
+            out_ref[row : row + unit_ref.shape[0], :] = unit_ref[...]
+            row += unit_ref.shape[0]
+
+
+def load_kernel(turned, *refs):
+    count = len(turned)
+    sources, targets, scratches, sems = refs[:count], refs[count : 2 * count], refs[2 * count : -1], refs[-1]
+    landing = list(scratches)
+    places = [landing.pop(0) if turn else target for turn, target in zip(turned, targets)]
+    copies = [pltpu.make_async_copy(a, b, sems.at[n]) for n, (a, b) in enumerate(zip(sources, places))]
     for copy in copies:
         copy.start()
-    copies[0].wait()
-    wkt_ref[...] = wk_ref[...].T
-    for copy in copies[1:]:
+    for copy, turn, place, target in zip(copies, turned, places, targets):
         copy.wait()
+        if turn:
+            target[...] = place[...].T
 
 
 def project_kernel(
@@ -105,11 +105,7 @@
         total += gap * gap
     inverse = lax.rsqrt(jnp.sum(total, axis=1, keepdims=True) * (1.0 / chans) + 1e-05)
 
-    row = lax.broadcasted_iota(jnp.int32, (256, 256), 0) // HD
-    col = lax.broadcasted_iota(jnp.int32, (256, 256), 1) // HD
-    same_head = jnp.where(row == col, 1.0, 0.0).astype(BF16)
-
-    per = 2
+    per = len(pieces)
     token_sum = jnp.zeros((1, width), F32)
     for i in range(0, len(pieces), per):
         places = [pl.ds(pl.multiple_of(b * LB, LB), LB) for b in blocks[i : i + per]]
@@ -123,16 +119,12 @@
         token_sum += jnp.sum(tokens, axis=0, keepdims=True)
         for n, at in enumerate(places):
             tokens_ref[at, :] = tokens[n * LB : (n + 1) * LB]
-        for c in range(width // 256):
-            part = slice(c * 256, (c + 1) * 256)
-            q = dot(normed, wq_ref[:, part])
-            squares = q * q
-            high = squares.astype(BF16)
-            low = (squares - high.astype(F32)).astype(BF16)
-            length = dot(high, same_head) + dot(low, same_head)
-            q = (q * lax.rsqrt(length + 1e-06)).astype(BF16)
-            for n, at in enumerate(places):
-                q_ref[at, part] = q[n * LB : (n + 1) * LB]
+        qt = lax.dot_general(wq_ref[...], normed, (((0,), (1,)), ((), ())), preferred_element_type=F32)
+        qt = qt.reshape(HEADS, HD, per * LB)
+        length = jnp.sum(qt * qt, axis=1, keepdims=True)
+        q = (qt * lax.rsqrt(length + 1e-06)).astype(BF16).reshape(width, per * LB).T
+        for n, at in enumerate(places):
+            q_ref[at, :] = q[n * LB : (n + 1) * LB]
         kt = dot_last(wkt_ref[...], normed)
         kt = kt.reshape(HEADS, HD, per * LB)
         length = jnp.sum(kt * kt, axis=1, keepdims=True)
@@ -146,8 +138,8 @@
 
 def attend_kernel(
     pattern_ref, scale_ref, q_ref, kt_ref, v_ref, sum_ref, wo_hbm, wproj_hbm,
-    heads_ref, proj_ref,
-    wo_ref, wproj_ref, sems,
+    heads_ref, proj_ref, wo_ref,
+    wproj_ref, sems,
 ):
     chans, width = q_ref.shape
     nblocks = chans // LB
@@ -191,7 +183,7 @@
             parts.append(jnp.sum(out.astype(F32), axis=0, keepdims=True))
         return heads_sum + jnp.concatenate(parts, axis=1)
 
-    heads_sum = lax.fori_loop(0, nblocks, attend, jnp.zeros((1, width), F32))
+    heads_sum = lax.fori_loop(0, nblocks, attend, jnp.zeros((1, width), F32), unroll=True)
 
     heads_mean = heads_sum * (1.0 / chans)
     first = heads_mean.astype(BF16)
@@ -207,7 +199,20 @@
     proj_ref[...] = dot(pooled, wproj_ref[...])[:1]
 
 
-def spread_kernel(place_ref, proj_ref, even_ref, odd_ref, mix_ref, first_ref, own_ref, second_ref):
+def layer_kernel(tokens_ref, heads_ref, wo_ref, layer_hbm, done_ref, rounded_ref, sems):
+    rows = tokens_ref.shape[0] // sems.shape[0]
+    copies = []
+    for n in range(sems.shape[0]):
+        at = pl.ds(n * rows, rows)
+        rounded_ref[at, :] = (tokens_ref[at, :] + dot(heads_ref[at, :], wo_ref[...])).astype(BF16)
+        copies.append(pltpu.make_async_copy(rounded_ref.at[at], layer_hbm.at[at], sems.at[n]))
+        copies[-1].start()
+    done_ref[...] = jnp.zeros(done_ref.shape, F32)
+    for copy in copies:
+        copy.wait()
+
+
+def spread_kernel(place_ref, proj_ref, even_ref, odd_ref, mix_ref, done_ref, first_ref, own_ref, second_ref):
     column_odd, row_odd = place_ref[0] & 1 != 0, place_ref[1] & 1 != 0
     before = jnp.where(column_odd, even_ref[...], odd_ref[...])
     after = jnp.where(column_odd, odd_ref[...], even_ref[...])
@@ -264,16 +269,16 @@
     return pltpu.CompilerParams(vmem_limit_bytes=mib * MIB)
 
 
-def load(pos_embed, w_in, w_query, w_key, w_value):
-    weights = (pos_embed, w_in, w_query, w_key, w_value)
+def load(turned, *weights):
     return pl.pallas_call(
-        load_kernel,
+        functools.partial(load_kernel, turned),
         out_shape=tuple(jax.ShapeDtypeStruct(w.shape, BF16) for w in weights),
-        in_specs=[ANY] * 5,
-        out_specs=(VMEM,) * 5,
-        scratch_shapes=[pltpu.VMEM(w_key.shape, BF16), pltpu.SemaphoreType.DMA((5,))],
-        compiler_params=vmem(16),
-        cost_estimate=pl.CostEstimate(flops=0, bytes_accessed=14_000_000, transcendentals=0),
+        in_specs=[ANY] * len(weights),
+        out_specs=(VMEM,) * len(weights),
+        scratch_shapes=[pltpu.VMEM(w.shape, BF16) for w, turn in zip(weights, turned) if turn]
+        + [pltpu.SemaphoreType.DMA((len(weights),))],
+        compiler_params=vmem(12),
+        cost_estimate=pl.CostEstimate(flops=0, bytes_accessed=sum(4 * w.size for w in weights), transcendentals=0),
     )(*weights)
 
 
@@ -302,12 +307,11 @@
         out_shape=(
             jax.ShapeDtypeStruct((chans, width), BF16),
             jax.ShapeDtypeStruct((1, w_proj.shape[1]), F32),
+            jax.ShapeDtypeStruct(w_out.shape, BF16),
         ),
         in_specs=[SMEM, SMEM, VMEM, VMEM, VMEM, VMEM, ANY, ANY],
-        out_specs=(VMEM, VMEM),
-        scratch_shapes=[
-            pltpu.VMEM(w_out.shape, BF16), pltpu.VMEM(w_proj.shape, BF16), pltpu.SemaphoreType.DMA((2,))
-        ],
+        out_specs=(VMEM,) * 3,
+        scratch_shapes=[pltpu.VMEM(w_proj.shape, BF16), pltpu.SemaphoreType.DMA((2,))],
         compiler_params=vmem(40),
         cost_estimate=pl.CostEstimate(flops=8_000_000_000, bytes_accessed=8_000_000, transcendentals=5_000_000),
     )(choose, attn_scale, queries, keys, values, token_sum, w_out, w_proj)
@@ -352,9 +356,10 @@
         compiler_params=vmem(8),
     )(place, cube, optical)
     far = other_half(far)
-    far, *weights = lax.optimization_barrier((far, pos_embed, w_in, w_query, w_key, w_value))
     unit = jnp.concatenate([unit, lax.ppermute(unit, "sy", [(i, i ^ 1) for i in range(nsy)])], axis=0)
     units = [unit] + [lax.ppermute(unit, "sy", [(i, (i + 2 * d) % nsy) for i in range(nsy)]) for d in range(1, nsy // 2)]
+    far, *weights = lax.optimization_barrier((far, pos_embed, w_in, w_query, w_key, w_value))
+    weights = load((False, False, False, True, False), *weights)
     sent = pl.pallas_call(
         merge_kernel,
         out_shape=(jax.ShapeDtypeStruct((2 * pixels + nsy * rows, LB), BF16),) * (half - 1),
@@ -363,21 +368,25 @@
         compiler_params=vmem(8),
     )(near, far, *units)
     taken = [steps_y(array, d) for d, array in enumerate(sent, 1)]
-
     candidates = jnp.concatenate(units + [array[2 * pixels :] for array in taken], axis=0)
     others = other_half(candidates)
-    tokens, queries, keys, values, token_sum = project(
-        place, [near, far] + taken, norm_gain, load(*weights)
-    )
+    tokens, queries, keys, values, token_sum = project(place, [near, far] + taken, norm_gain, weights)
     others, token_sum = lax.optimization_barrier((others, token_sum))
     candidates = jnp.concatenate([candidates, others], axis=0)
     candidates = [candidates] + [
         lax.ppermute(candidates, "sx", [(i, (i + d) % nsx) for i in range(nsx)]) for d in range(1, nsx)
     ]
     choose = pattern.reshape(pattern.shape[3], pattern.shape[4])
-    heads_out, proj = attend(choose, attn_scale, queries, keys, values, token_sum, w_out, w_proj)
-    proj, *candidates = lax.optimization_barrier((proj, *candidates))
-    layer_out = (tokens + dot(heads_out, w_out)).astype(BF16)
+    heads_out, proj, held_out = attend(choose, attn_scale, queries, keys, values, token_sum, w_out, w_proj)
+    layer_out, done = pl.pallas_call(
+        layer_kernel,
+        out_shape=(jax.ShapeDtypeStruct(tokens.shape, BF16), jax.ShapeDtypeStruct((8, LB), F32)),
+        in_specs=[VMEM] * 3,
+        out_specs=(ANY, VMEM),
+        scratch_shapes=[pltpu.VMEM(tokens.shape, BF16), pltpu.SemaphoreType.DMA((4,))],
+        compiler_params=vmem(16),
+        cost_estimate=pl.CostEstimate(flops=2_000_000_000, bytes_accessed=8_000_000, transcendentals=0),
+    )(tokens, heads_out, held_out)
 
     even = lax.ppermute(proj, ("freq", "sx"), column_pairs(0, nfreq, nsx))
     odd = lax.ppermute(proj, ("freq", "sx"), column_pairs(1, nfreq, nsx))
@@ -385,10 +394,10 @@
     first, own, second = pl.pallas_call(
         spread_kernel,
         out_shape=(line,) * 3,
-        in_specs=[SMEM] + [VMEM] * 4,
+        in_specs=[SMEM] + [VMEM] * 5,
         out_specs=(VMEM,) * 3,
         compiler_params=vmem(4),
-    )(place, proj, even, odd, mix_weight)
+    )(place, proj, even, odd, mix_weight, done)
     first = lax.ppermute(first, "sy", pairs(nsy, 0))
     second = lax.ppermute(second, "sy", pairs(nsy, 1))
     embed, loss = pl.pallas_call(

time: 86.9 us -> 80.2 us (0.923)
  waiting for transfers between devices: 7.02 us -> 12 us
  starting transfers between devices: 42.3 us -> 37.8 us
  Pallas kernels: 23.7 us -> 19.4 us
  other arithmetic: 1.69 us -> 0.08 us
  matrix products: 1.39 us -> 0 us
    pallas_call x1, Pallas kernels: 9.59 us -> 5.66 us  [project(): pl.pallas_call(project_kernel, out_shape=(jax.ShapeDtypeStruct((chans, wi...]
    pallas_call x1, Pallas kernels: 9.24 us -> 6.68 us  [attend(): pl.pallas_call(attend_kernel, out_shape=(jax.ShapeDtypeStruct((chans, wid...]
    pallas_call x1 -> x2, Pallas kernels: 1.42 us -> 3.65 us  [the longest x1 2.23 us: per_device(): pl.pallas_call(layer_kernel, out_shape=(jax.ShapeDtypeStruct(tokens.shape...]
    ppermute x1, starting transfers between devices: 9.51 us -> 7.38 us  [per_device(): odd = lax.ppermute(proj, ('freq', 'sx'), column_pairs(1, nfreq, nsx))]
    ppermute x2, waiting for transfers between devices: 0.01 us -> 1.82 us  [other_half(): lax.ppermute(array, 'freq', [(i, (i + half) % nfreq) for i in range(nfreq)])]
    reshape x1 -> x0, other arithmetic: 1.62 us -> none  [per_device(): layer_out.reshape((1, 1, 1) + layer_out.shape)]
    dot_general x1 -> x0, matrix products: 1.39 us -> none  [dot(): return jnp.dot(a, b, preferred_element_type=F32)]
    ppermute x3, waiting for transfers between devices: 6.69 us -> 8.08 us  [per_device(): lax.ppermute(unit, 'sy', [(i, (i + 2 * d) % nsy) for i in range(nsy)])]
  transfers between devices with their start and end apart: 16 -> 16, of which waited for: 3 -> 5; matrix products, arithmetic and copies ran while one was open for 5% -> 2% of each run, Pallas kernels for 23% -> 21%
where the time goes in v2:
time: 80.2 us; the launch traced here: 79.8 us
  starting transfers between devices  37.8 us (47%)
  Pallas kernels  19.4 us (24%)
  waiting for transfers between devices  12 us (15%)
  local copies, waits for them, and re-layouts  8.32 us (10%)
  between operations  2.1 us (3%)
    ppermute x3, waiting for transfers between devices, per_device(): lax.ppermute(unit, 'sy', [(i, (i + 2 * d) % nsy) for i in range(nsy)])  8.08 us
    ppermute x1, starting transfers between devices, per_device(): odd = lax.ppermute(proj, ('freq', 'sx'), column_pairs(1, nfreq, nsx))  7.38 us
    ppermute x2, starting transfers between devices, other_half(): lax.ppermute(array, 'freq', [(i, (i + half) % nfreq) for i in range(nfreq)])  7.27 us
    unnamed x30, local copies, waits for them, and re-layouts  6.86 us
    pallas_call x1, Pallas kernels, attend(): pl.pallas_call(attend_kernel, out_shape=(jax.ShapeDtypeStruct((chans, wid...  6.68 us
    ppermute x1, starting transfers between devices, per_device(): first = lax.ppermute(first, 'sy', pairs(nsy, 0))  6.39 us
    pallas_call x1, Pallas kernels, project(): pl.pallas_call(project_kernel, out_shape=(jax.ShapeDtypeStruct((chans, wi...  5.66 us
    ppermute x3, starting transfers between devices, steps_y(): lax.ppermute(array, 'freq', [(i, i // half * half + (i + d) % half) for i...  5.14 us
  transfers between devices with their start and end apart: 16, of which 5 were waited for; matrix products, arithmetic and copies ran while one was open for 2% of the time, Pallas kernels for 21%

profile of v2, /device:TPU:3, one launch (start us, length us, event | category | flops | bytes accessed | tf_op | source)
XLA Modules:
  0.0 79.8 jit_solution(15067202510085047221)
XLA Ops:
  0.7 1.1 %copy-done.4 = bf16[128,16,128]{2,1,0:T(8,128)(2,1)S(1)} copy-done((bf16[128,16,128]{2,1,0:T(8,128)(2,1)S(1)}, bf16[128,16,128]{2,1,0:T(8,128)(2,1)}, u32[]{:S(2)}) %copy-start.4) | copy-done | bytes 524312
  1.8 0.7 copy-done.7
  2.5 1.0 %shard_map.166 = (bf16[4,256,128]{2,1,0:T(8,128)(2,1)S(1)}, bf16[4,256,128]{2,1,0:T(8,128)(2,1)S(1)}, bf16[16,128]{1,0:T(8,128)(2,1)S(1)}) custom-call(s32[3]{0:T(128)S(1)} %pad_add_fusion.place_ref, bf16[128,16,128]{2,1,0:T(8,128)(2,1)S(1)} %copy-done.4, bf16[4,512]{1,0:T(4,128)(2,1)S(1)} %copy-done.7), custom_call_target="tpu_custom_call" | custom-call | tf_op jit(solution)/shard_map/pallas_call | solution.py:350
  3.5 0.8 collective-permute-start.1
  4.3 6.9 %collective-permute-start = (bf16[4,256,128]{2,1,0:T(8,128)(2,1)S(1)}, bf16[4,256,128]{2,1,0:T(8,128)(2,1)S(1)}, u32[]{:S(2)}, u32[]{:S(2)}) collective-permute-start(bf16[4,256,128]{2,1,0:T(8,128)(2,1)S(1)} %get-tuple-element.38), channel_id=1, source_target_pairs={{0,128},{32,160},{64,192},{96,224},{128,0},{160,32},{192,64},{224,... | collective-permute-start | bytes 786440 | tf_op jit(solution)/shard_map/ppermute | solution.py:347
  11.2 0.8 %collective-permute-start.2 = (bf16[32,128]{1,0:T(8,128)(2,1)S(1)}, bf16[32,128]{1,0:T(8,128)(2,1)S(1)}, u32[]{:S(2)}, u32[]{:S(2)}) collective-permute-start(bf16[32,128]{1,0:T(8,128)(2,1)S(1)} %get-tuple-element.85.refs_0_), channel_id=1, source_target_pairs={{0,8},{4,12},{8,16},{12,20},{16,24},{20,28},{24,0},{28,4},{1,9},{5... | collective-permute-start | bytes 24584 | tf_op jit(solution)/shard_map/ppermute | solution.py:360
  12.1 0.7 reshape.24.gain_ref
  12.8 0.8 copy.19
  13.5 1.2 %collective-permute-start.3 = (bf16[32,128]{1,0:T(8,128)(2,1)S(1)}, bf16[32,128]{1,0:T(8,128)(2,1)S(1)}, u32[]{:S(2)}, u32[]{:S(2)}) collective-permute-start(bf16[32,128]{1,0:T(8,128)(2,1)S(1)} %get-tuple-element.85.refs_0_), channel_id=1, source_target_pairs={{0,16},{4,20},{8,24},{12,28},{16,0},{20,4},{24,8},{28,12},{1,17},{... | collective-permute-start | bytes 24584 | tf_op jit(solution)/shard_map/ppermute | solution.py:360
  14.7 1.6 %collective-permute-start.4 = (bf16[32,128]{1,0:T(8,128)(2,1)S(1)}, bf16[32,128]{1,0:T(8,128)(2,1)S(1)}, u32[]{:S(2)}, u32[]{:S(2)}) collective-permute-start(bf16[32,128]{1,0:T(8,128)(2,1)S(1)} %get-tuple-element.85.refs_0_), channel_id=1, source_target_pairs={{0,24},{4,28},{8,0},{12,4},{16,8},{20,12},{24,16},{28,20},{1,25},{... | collective-permute-start | bytes 24584 | tf_op jit(solution)/shard_map/ppermute | solution.py:360
  16.3 6.7 %collective-permute-done.2.refs_1_ = bf16[32,128]{1,0:T(8,128)(2,1)S(1)} collective-permute-done((bf16[32,128]{1,0:T(8,128)(2,1)S(1)}, bf16[32,128]{1,0:T(8,128)(2,1)S(1)}, u32[]{:S(2)}, u32[]{:S(2)}) %collective-permute-start.2) | collective-permute-done | bytes 8224 | tf_op jit(solution)/shard_map/ppermute | solution.py:360
  23.1 1.3 %collective-permute-done.4.refs_3_ = bf16[32,128]{1,0:T(8,128)(2,1)S(1)} collective-permute-done((bf16[32,128]{1,0:T(8,128)(2,1)S(1)}, bf16[32,128]{1,0:T(8,128)(2,1)S(1)}, u32[]{:S(2)}, u32[]{:S(2)}) %collective-permute-start.4) | collective-permute-done | bytes 8224 | tf_op jit(solution)/shard_map/ppermute | solution.py:360
  24.5 1.4 %collective-permute-start.5 = (bf16[640,128]{1,0:T(8,128)(2,1)S(1)}, bf16[640,128]{1,0:T(8,128)(2,1)S(1)}, u32[]{:S(2)}, u32[]{:S(2)}) collective-permute-start(bf16[640,128]{1,0:T(8,128)(2,1)S(1)} %get-tuple-element.41), channel_id=1, source_target_pairs={{0,32},{32,64},{64,96},{96,0},{128,160},{160,192},{192,224},{224,1... | collective-permute-start | bytes 491528 | tf_op jit(solution)/shard_map/ppermute | solution.py:344
  25.9 2.7 %collective-permute-start.6 = (bf16[640,128]{1,0:T(8,128)(2,1)S(1)}, bf16[640,128]{1,0:T(8,128)(2,1)S(1)}, u32[]{:S(2)}, u32[]{:S(2)}) collective-permute-start(bf16[640,128]{1,0:T(8,128)(2,1)S(1)} %get-tuple-element.42), channel_id=1, source_target_pairs={{0,64},{32,96},{64,0},{96,32},{128,192},{160,224},{192,128},{224,1... | collective-permute-start | bytes 491528 | tf_op jit(solution)/shard_map/ppermute | solution.py:344
  28.6 1.1 %collective-permute-start.7 = (bf16[640,128]{1,0:T(8,128)(2,1)S(1)}, bf16[640,128]{1,0:T(8,128)(2,1)S(1)}, u32[]{:S(2)}, u32[]{:S(2)}) collective-permute-start(bf16[640,128]{1,0:T(8,128)(2,1)S(1)} %get-tuple-element.43), channel_id=1, source_target_pairs={{0,96},{32,0},{64,32},{96,64},{128,224},{160,128},{192,160},{224,1... | collective-permute-start | bytes 491528 | tf_op jit(solution)/shard_map/ppermute | solution.py:344
  29.6 1.4 %copy-done = bf16[1024,768]{1,0:T(8,128)(2,1)S(1)} copy-done((bf16[1024,768]{1,0:T(8,128)(2,1)S(1)}, bf16[1024,768]{1,0:T(8,128)(2,1)}, u32[]{:S(2)}) %copy-start) | copy-done | bytes 1572888
  31.0 1.3 %copy-done.2 = bf16[768,768]{1,0:T(8,128)(2,1)S(1)} copy-done((bf16[768,768]{1,0:T(8,128)(2,1)S(1)}, bf16[768,768]{1,0:T(8,128)(2,1)}, u32[]{:S(2)}) %copy-start.2) | copy-done | bytes 1179672
  32.3 1.3 %copy-done.3 = bf16[768,768]{1,0:T(8,128)(2,1)S(1)} copy-done((bf16[768,768]{1,0:T(8,128)(2,1)S(1)}, bf16[768,768]{1,0:T(8,128)(2,1)}, u32[]{:S(2)}) %copy-start.3) | copy-done | bytes 1179672
  33.6 1.0 %copy-done.5 = bf16[256,768]{1,0:T(8,128)(2,1)S(1)} copy-done((bf16[256,768]{1,0:T(8,128)(2,1)S(1)}, bf16[256,768]{1,0:T(8,128)(2,1)}, u32[]{:S(2)}) %copy-start.5) | copy-done | bytes 393240
  34.6 1.4 %shard_map.168 = (bf16[1024,768]{1,0:T(8,128)(2,1)S(1)}, bf16[256,768]{1,0:T(8,128)(2,1)S(1)}, bf16[768,768]{1,0:T(8,128)(2,1)S(1)}, bf16[768,768]{1,0:T(8,128)(2,1)S(1)}, bf16[768,768]{1,0:T(8,128)(2,1)S(1)}) custom-call(bf16[1024,768]{1,0:T(8,128)(2,1)S(1)} %copy-done, bf16[256,768]{1,0:T(8,128)(2,1)S(1)} %copy-done.5, bf16[768,768]{1,0:T(8,128)(2,1)S(1)} %copy-done.1, ...), custom_call_target="tpu_custom_call" | custom-call | bytes 11010048 | tf_op jit(solution)/shard_map/pallas_call | solution.py:273
  36.4 5.7 %shard_map.169 = (f32[1024,768]{1,0:T(8,128)S(1)}, bf16[1024,768]{1,0:T(8,128)(2,1)S(1)}, bf16[8,768,128]{2,1,0:T(8,128)(2,1)S(1)}, bf16[1024,768]{1,0:T(8,128)(2,1)S(1)}, f32[1,768]{1,0:T(1,128)S(1)}) custom-call(s32[3]{0:T(128)S(1)} %pad_add_fusion.place_ref, bf16[4,256,128]{2,1,0:T(8,128)(2,1)S(1)} %get-tuple-element.37.near_ref, ...), custom_call_target="tpu_custom_call" | custom-call | flops 8000000000 | bytes 12000000 | tf_op jit(solution)/shard_map/pallas_call | solution.py:287
  42.1 1.8 %collective-permute-done.8 = bf16[512,128]{1,0:T(8,128)(2,1)S(1)} collective-permute-done((bf16[512,128]{1,0:T(8,128)(2,1)S(1)}, bf16[512,128]{1,0:T(8,128)(2,1)S(1)}, u32[]{:S(2)}, u32[]{:S(2)}) %collective-permute-start.8) | collective-permute-done | bytes 131104 | tf_op jit(solution)/shard_map/ppermute | solution.py:347
  44.0 1.5 %collective-permute-start.13 = (bf16[1024,128]{1,0:T(8,128)(2,1)S(1)}, bf16[1024,128]{1,0:T(8,128)(2,1)S(1)}, u32[]{:S(2)}, u32[]{:S(2)}) collective-permute-start(bf16[1024,128]{1,0:T(8,128)(2,1)S(1)} %constant_dynamic-update-slice_fusion.10.refs_0_), channel_id=1, source_target_pairs={{0,1},{1,2},{2,3},{3,0},{4,5},{5,6},{6,7},{7,4},{8,9},{9,10},{10,1... | collective-permute-start | bytes 786440 | tf_op jit(solution)/shard_map/ppermute | solution.py:377
  45.4 0.8 %collective-permute-start.14 = (bf16[1024,128]{1,0:T(8,128)(2,1)S(1)}, bf16[1024,128]{1,0:T(8,128)(2,1)S(1)}, u32[]{:S(2)}, u32[]{:S(2)}) collective-permute-start(bf16[1024,128]{1,0:T(8,128)(2,1)S(1)} %constant_dynamic-update-slice_fusion.10.refs_0_), channel_id=1, source_target_pairs={{0,2},{1,3},{2,0},{3,1},{4,6},{5,7},{6,4},{7,5},{8,10},{9,11},{10,... | collective-permute-start | bytes 786440 | tf_op jit(solution)/shard_map/ppermute | solution.py:377
  46.3 1.9 %collective-permute-start.15 = (bf16[1024,128]{1,0:T(8,128)(2,1)S(1)}, bf16[1024,128]{1,0:T(8,128)(2,1)S(1)}, u32[]{:S(2)}, u32[]{:S(2)}) collective-permute-start(bf16[1024,128]{1,0:T(8,128)(2,1)S(1)} %constant_dynamic-update-slice_fusion.10.refs_0_), channel_id=1, source_target_pairs={{0,3},{1,0},{2,1},{3,2},{4,7},{5,4},{6,5},{7,6},{8,11},{9,8},{10,9... | collective-permute-start | bytes 786440 | tf_op jit(solution)/shard_map/ppermute | solution.py:377
  48.1 6.7 %shard_map.170 = (bf16[1024,768]{1,0:T(8,128)(2,1)S(1)}, f32[1,512]{1,0:T(1,128)S(1)}, bf16[768,768]{1,0:T(8,128)(2,1)S(1)}) custom-call(s32[8,3]{1,0:T(8,128)S(1)} %bitcast.9, f32[12]{0:T(128)S(1)} %copy-done.10, bf16[1024,768]{1,0:T(8,128)(2,1)S(1)} %get-tuple-element.55.q_ref, bf16[8,768,128]{2,1,0:T(8,128)(2,1)S(1)} %get-tuple-element.56.kt_ref, ...), custom_call_target="tpu_custom_call" | custom-call | flops 8000000000 | bytes 8000000 | tf_op jit(solution)/shard_map/pallas_call | solution.py:305
  54.8 7.4 %collective-permute-start.10 = (f32[1,512]{1,0:T(1,128)S(1)}, f32[1,512]{1,0:T(1,128)S(1)}, u32[]{:S(2)}, u32[]{:S(2)}) collective-permute-start(f32[1,512]{1,0:T(1,128)S(1)} %get-tuple-element.63.proj_ref), channel_id=1, source_target_pairs={{32,64},{64,32},{96,128},{128,96},{160,192},{192,160},{224,1},{1,2... | collective-permute-start | bytes 6152 | tf_op jit(solution)/shard_map/ppermute | solution.py:392
  62.3 2.2 %shard_map.171 = (bf16[1024,768]{1,0:T(8,128)(2,1)}, f32[8,128]{1,0:T(8,128)S(1)}) custom-call(f32[1024,768]{1,0:T(8,128)S(1)} %get-tuple-element.54.tokens_ref, bf16[1024,768]{1,0:T(8,128)(2,1)S(1)} %get-tuple-element.60.heads_ref, bf16[768,768]{1,0:T(8,128)(2,1)S(1)} %get-tuple-element.61.wo_ref), custom_call_target="tpu_custom_call" | custom-call | flops 2000000000 | bytes 8000000 | tf_op jit(solution)/shard_map/pallas_call | solution.py:381
  64.6 1.5 %collective-permute-done.10.odd_ref = f32[1,512]{1,0:T(1,128)S(1)} collective-permute-done((f32[1,512]{1,0:T(1,128)S(1)}, f32[1,512]{1,0:T(1,128)S(1)}, u32[]{:S(2)}, u32[]{:S(2)}) %collective-permute-start.10) | collective-permute-done | bytes 2080 | tf_op jit(solution)/shard_map/ppermute | solution.py:392
  66.6 6.4 %collective-permute-start.11 = (f32[1,512]{1,0:T(1,128)S(1)}, f32[1,512]{1,0:T(1,128)S(1)}, u32[]{:S(2)}, u32[]{:S(2)}) collective-permute-start(f32[1,512]{1,0:T(1,128)S(1)} %get-tuple-element.65), channel_id=1, source_target_pairs={{0,4},{4,0},{8,12},{12,8},{16,20},{20,16},{24,28},{28,24},{1,5},{5... | collective-permute-start | bytes 6152 | tf_op jit(solution)/shard_map/ppermute | solution.py:401
  73.0 3.0 %collective-permute-start.12 = (f32[1,512]{1,0:T(1,128)S(1)}, f32[1,512]{1,0:T(1,128)S(1)}, u32[]{:S(2)}, u32[]{:S(2)}) collective-permute-start(f32[1,512]{1,0:T(1,128)S(1)} %get-tuple-element.67), channel_id=1, source_target_pairs={{4,8},{8,4},{12,16},{16,12},{20,24},{24,20},{5,9},{9,5},{13,17},{1... | collective-permute-start | bytes 6152 | tf_op jit(solution)/shard_map/ppermute | solution.py:402
  77.9 1.9 %shard_map.173 = (f32[1,512]{1,0:T(1,128)}, f32[1,1]{1,0:T(1,128)}) custom-call(s32[3]{0:T(128)S(1)} %pad_add_fusion.place_ref, f32[1]{0:T(128)S(6)} %copy.36.scale_ref, s32[1]{0:T(128)} %bitcast.8.target_ref, f32[1,512]{1,0:T(1,128)S(1)} %collective-permute-done.11.first_ref, f32[1,512]{1,0:T(1,128)S(1)} %get-tuple-element.66.own_ref, ...), custom_call_target="tpu_custom_call" | custom-call | tf_op jit(solution)/shard_map/pallas_call | solution.py:403
  (42 shorter events, 1.9 us)
Async XLA Ops:
  0.6 29.0 %copy-start.1 = (bf16[768,768]{1,0:T(8,128)(2,1)S(1)}, bf16[768,768]{1,0:T(8,128)(2,1)}, u32[]{:S(2)}) copy-start(bf16[768,768]{1,0:T(8,128)(2,1)} %refs_2_) | copy-start | bytes 3538948
  0.7 1.1 %copy-start.4 = (bf16[128,16,128]{2,1,0:T(8,128)(2,1)S(1)}, bf16[128,16,128]{2,1,0:T(8,128)(2,1)}, u32[]{:S(2)}) copy-start(bf16[128,16,128]{2,1,0:T(8,128)(2,1)} %cube_ref.1) | copy-start | bytes 1572868
  1.8 0.7 copy-start.7
  3.5 7.7 %collective-permute-start.1 = (bf16[16,128]{1,0:T(8,128)(2,1)S(1)}, bf16[16,128]{1,0:T(8,128)(2,1)S(1)}, u32[]{:S(2)}, u32[]{:S(2)}) collective-permute-start(bf16[16,128]{1,0:T(8,128)(2,1)S(1)} %get-tuple-element.40), channel_id=1, source_target_pairs={{0,4},{4,0},{8,12},{12,8},{16,20},{20,16},{24,28},{28,24},{1,5},{5... | collective-permute-start | bytes 12296 | tf_op jit(solution)/shard_map/ppermute | solution.py:359
  4.3 18.8 %collective-permute-start = (bf16[4,256,128]{2,1,0:T(8,128)(2,1)S(1)}, bf16[4,256,128]{2,1,0:T(8,128)(2,1)S(1)}, u32[]{:S(2)}, u32[]{:S(2)}) collective-permute-start(bf16[4,256,128]{2,1,0:T(8,128)(2,1)S(1)} %get-tuple-element.38), channel_id=1, source_target_pairs={{0,128},{32,160},{64,192},{96,224},{128,0},{160,32},{192,64},{224,... | collective-permute-start | bytes 786440 | tf_op jit(solution)/shard_map/ppermute | solution.py:347
  11.2 11.8 %collective-permute-start.2 = (bf16[32,128]{1,0:T(8,128)(2,1)S(1)}, bf16[32,128]{1,0:T(8,128)(2,1)S(1)}, u32[]{:S(2)}, u32[]{:S(2)}) collective-permute-start(bf16[32,128]{1,0:T(8,128)(2,1)S(1)} %get-tuple-element.85.refs_0_), channel_id=1, source_target_pairs={{0,8},{4,12},{8,16},{12,20},{16,24},{20,28},{24,0},{28,4},{1,9},{5... | collective-permute-start | bytes 24584 | tf_op jit(solution)/shard_map/ppermute | solution.py:360
  13.5 9.6 %collective-permute-start.3 = (bf16[32,128]{1,0:T(8,128)(2,1)S(1)}, bf16[32,128]{1,0:T(8,128)(2,1)S(1)}, u32[]{:S(2)}, u32[]{:S(2)}) collective-permute-start(bf16[32,128]{1,0:T(8,128)(2,1)S(1)} %get-tuple-element.85.refs_0_), channel_id=1, source_target_pairs={{0,16},{4,20},{8,24},{12,28},{16,0},{20,4},{24,8},{28,12},{1,17},{... | collective-permute-start | bytes 24584 | tf_op jit(solution)/shard_map/ppermute | solution.py:360
  14.7 9.7 %collective-permute-start.4 = (bf16[32,128]{1,0:T(8,128)(2,1)S(1)}, bf16[32,128]{1,0:T(8,128)(2,1)S(1)}, u32[]{:S(2)}, u32[]{:S(2)}) collective-permute-start(bf16[32,128]{1,0:T(8,128)(2,1)S(1)} %get-tuple-element.85.refs_0_), channel_id=1, source_target_pairs={{0,24},{4,28},{8,0},{12,4},{16,8},{20,12},{24,16},{28,20},{1,25},{... | collective-permute-start | bytes 24584 | tf_op jit(solution)/shard_map/ppermute | solution.py:360
  24.5 11.5 %collective-permute-start.5 = (bf16[640,128]{1,0:T(8,128)(2,1)S(1)}, bf16[640,128]{1,0:T(8,128)(2,1)S(1)}, u32[]{:S(2)}, u32[]{:S(2)}) collective-permute-start(bf16[640,128]{1,0:T(8,128)(2,1)S(1)} %get-tuple-element.41), channel_id=1, source_target_pairs={{0,32},{32,64},{64,96},{96,0},{128,160},{160,192},{192,224},{224,1... | collective-permute-start | bytes 491528 | tf_op jit(solution)/shard_map/ppermute | solution.py:344
  25.9 10.2 %collective-permute-start.6 = (bf16[640,128]{1,0:T(8,128)(2,1)S(1)}, bf16[640,128]{1,0:T(8,128)(2,1)S(1)}, u32[]{:S(2)}, u32[]{:S(2)}) collective-permute-start(bf16[640,128]{1,0:T(8,128)(2,1)S(1)} %get-tuple-element.42), channel_id=1, source_target_pairs={{0,64},{32,96},{64,0},{96,32},{128,192},{160,224},{192,128},{224,1... | collective-permute-start | bytes 491528 | tf_op jit(solution)/shard_map/ppermute | solution.py:344
  28.6 7.5 %collective-permute-start.7 = (bf16[640,128]{1,0:T(8,128)(2,1)S(1)}, bf16[640,128]{1,0:T(8,128)(2,1)S(1)}, u32[]{:S(2)}, u32[]{:S(2)}) collective-permute-start(bf16[640,128]{1,0:T(8,128)(2,1)S(1)} %get-tuple-element.43), channel_id=1, source_target_pairs={{0,96},{32,0},{64,32},{96,64},{128,224},{160,128},{192,160},{224,1... | collective-permute-start | bytes 491528 | tf_op jit(solution)/shard_map/ppermute | solution.py:344
  29.6 1.4 %copy-start = (bf16[1024,768]{1,0:T(8,128)(2,1)S(1)}, bf16[1024,768]{1,0:T(8,128)(2,1)}, u32[]{:S(2)}) copy-start(bf16[1024,768]{1,0:T(8,128)(2,1)} %refs_0_) | copy-start | bytes 4718596
  31.0 1.3 %copy-start.2 = (bf16[768,768]{1,0:T(8,128)(2,1)S(1)}, bf16[768,768]{1,0:T(8,128)(2,1)}, u32[]{:S(2)}) copy-start(bf16[768,768]{1,0:T(8,128)(2,1)} %refs_3_) | copy-start | bytes 3538948
  32.3 1.3 %copy-start.3 = (bf16[768,768]{1,0:T(8,128)(2,1)S(1)}, bf16[768,768]{1,0:T(8,128)(2,1)}, u32[]{:S(2)}) copy-start(bf16[768,768]{1,0:T(8,128)(2,1)} %refs_4_) | copy-start | bytes 3538948
  33.6 1.0 %copy-start.5 = (bf16[256,768]{1,0:T(8,128)(2,1)S(1)}, bf16[256,768]{1,0:T(8,128)(2,1)}, u32[]{:S(2)}) copy-start(bf16[256,768]{1,0:T(8,128)(2,1)} %refs_1_) | copy-start | bytes 1179652
  36.1 7.8 %collective-permute-start.8 = (bf16[512,128]{1,0:T(8,128)(2,1)S(1)}, bf16[512,128]{1,0:T(8,128)(2,1)S(1)}, u32[]{:S(2)}, u32[]{:S(2)}) collective-permute-start(bf16[512,128]{1,0:T(8,128)(2,1)S(1)} %get-tuple-element.72), channel_id=1, source_target_pairs={{0,128},{32,160},{64,192},{96,224},{128,0},{160,32},{192,64},{224,... | collective-permute-start | bytes 393224 | tf_op jit(solution)/shard_map/ppermute | solution.py:347
  36.4 11.7 %copy-start.8 = (bf16[768,768]{1,0:T(8,128)(2,1)S(1)}, bf16[768,768]{1,0:T(8,128)(2,1)}, u32[]{:S(2)}) copy-start(bf16[768,768]{1,0:T(8,128)(2,1)} %wo_hbm.1) | copy-start | bytes 3538948
  36.4 11.7 %copy-start.9 = (bf16[768,512]{1,0:T(8,128)(2,1)S(1)}, bf16[768,512]{1,0:T(8,128)(2,1)}, u32[]{:S(2)}) copy-start(bf16[768,512]{1,0:T(8,128)(2,1)} %wproj_hbm.1) | copy-start | bytes 2359300
  36.4 11.7 %copy-start.10 = (f32[12]{0:T(128)S(1)}, f32[12]{0:T(128)}, u32[]{:S(2)}) copy-start(f32[12]{0:T(128)} %scale_ref.2) | copy-start | bytes 148
  44.0 34.0 %collective-permute-start.13 = (bf16[1024,128]{1,0:T(8,128)(2,1)S(1)}, bf16[1024,128]{1,0:T(8,128)(2,1)S(1)}, u32[]{:S(2)}, u32[]{:S(2)}) collective-permute-start(bf16[1024,128]{1,0:T(8,128)(2,1)S(1)} %constant_dynamic-update-slice_fusion.10.refs_0_), channel_id=1, source_target_pairs={{0,1},{1,2},{2,3},{3,0},{4,5},{5,6},{6,7},{7,4},{8,9},{9,10},{10,1... | collective-permute-start | bytes 786440 | tf_op jit(solution)/shard_map/ppermute | solution.py:377
  45.4 32.5 %collective-permute-start.14 = (bf16[1024,128]{1,0:T(8,128)(2,1)S(1)}, bf16[1024,128]{1,0:T(8,128)(2,1)S(1)}, u32[]{:S(2)}, u32[]{:S(2)}) collective-permute-start(bf16[1024,128]{1,0:T(8,128)(2,1)S(1)} %constant_dynamic-update-slice_fusion.10.refs_0_), channel_id=1, source_target_pairs={{0,2},{1,3},{2,0},{3,1},{4,6},{5,7},{6,4},{7,5},{8,10},{9,11},{10,... | collective-permute-start | bytes 786440 | tf_op jit(solution)/shard_map/ppermute | solution.py:377
  46.3 31.7 %collective-permute-start.15 = (bf16[1024,128]{1,0:T(8,128)(2,1)S(1)}, bf16[1024,128]{1,0:T(8,128)(2,1)S(1)}, u32[]{:S(2)}, u32[]{:S(2)}) collective-permute-start(bf16[1024,128]{1,0:T(8,128)(2,1)S(1)} %constant_dynamic-update-slice_fusion.10.refs_0_), channel_id=1, source_target_pairs={{0,3},{1,0},{2,1},{3,2},{4,7},{5,4},{6,5},{7,6},{8,11},{9,8},{10,9... | collective-permute-start | bytes 786440 | tf_op jit(solution)/shard_map/ppermute | solution.py:377
  54.8 11.2 %collective-permute-start.10 = (f32[1,512]{1,0:T(1,128)S(1)}, f32[1,512]{1,0:T(1,128)S(1)}, u32[]{:S(2)}, u32[]{:S(2)}) collective-permute-start(f32[1,512]{1,0:T(1,128)S(1)} %get-tuple-element.63.proj_ref), channel_id=1, source_target_pairs={{32,64},{64,32},{96,128},{128,96},{160,192},{192,160},{224,1},{1,2... | collective-permute-start | bytes 6152 | tf_op jit(solution)/shard_map/ppermute | solution.py:392
  62.2 3.9 %collective-permute-start.9 = (f32[1,512]{1,0:T(1,128)S(1)}, f32[1,512]{1,0:T(1,128)S(1)}, u32[]{:S(2)}, u32[]{:S(2)}) collective-permute-start(f32[1,512]{1,0:T(1,128)S(1)} %get-tuple-element.63.proj_ref), channel_id=1, source_target_pairs={{0,32},{32,0},{64,96},{96,64},{128,160},{160,128},{192,224},{224,1... | collective-permute-start | bytes 6152 | tf_op jit(solution)/shard_map/ppermute | solution.py:391
  62.3 3.8 %copy-start.6 = (f32[3,3,512]{2,1,0:T(4,128)S(1)}, f32[3,3,512]{2,1,0:T(4,128)}, u32[]{:S(2)}) copy-start(f32[3,3,512]{2,1,0:T(4,128)} %mix_ref.1) | copy-start | bytes 55300
  66.6 10.7 %collective-permute-start.11 = (f32[1,512]{1,0:T(1,128)S(1)}, f32[1,512]{1,0:T(1,128)S(1)}, u32[]{:S(2)}, u32[]{:S(2)}) collective-permute-start(f32[1,512]{1,0:T(1,128)S(1)} %get-tuple-element.65), channel_id=1, source_target_pairs={{0,4},{4,0},{8,12},{12,8},{16,20},{20,16},{24,28},{28,24},{1,5},{5... | collective-permute-start | bytes 6152 | tf_op jit(solution)/shard_map/ppermute | solution.py:401
  73.0 4.9 %collective-permute-start.12 = (f32[1,512]{1,0:T(1,128)S(1)}, f32[1,512]{1,0:T(1,128)S(1)}, u32[]{:S(2)}, u32[]{:S(2)}) collective-permute-start(f32[1,512]{1,0:T(1,128)S(1)} %get-tuple-element.67), channel_id=1, source_target_pairs={{4,8},{8,4},{12,16},{16,12},{20,24},{24,20},{5,9},{9,5},{13,17},{1... | collective-permute-start | bytes 6152 | tf_op jit(solution)/shard_map/ppermute | solution.py:402

commit v3 on v2

--- a/solution.py
+++ b/solution.py
@@ -31,7 +31,7 @@
     return lax.dot_general(a, b, (((1,), (1,)), ((), ())), preferred_element_type=F32)
 
 
-def pack_kernel(place_ref, cube_ref, optical_ref, near_ref, far_ref, unit_ref, wide_ref):
+def pack_kernel(place_ref, cube_ref, near_ref, far_ref, wide_ref):
     chans, side, columns = cube_ref.shape
     nfreq = columns // side
     half = nfreq // 2
@@ -46,6 +46,10 @@
             high = turned[(half + y) * side : (half + y + 1) * side, :]
             near_ref[d, at, :] = jnp.where(mine < half, low, high)
             far_ref[d, at, :] = jnp.where(mine < half, high, low)
+
+
+def unit_kernel(after_ref, optical_ref, unit_ref):
+    del after_ref
     optical = optical_ref[...].astype(F32)
     unit = (optical * lax.rsqrt(jnp.sum(optical * optical, axis=-1, keepdims=True) + 1e-06)).astype(BF16)
     unit_ref[...] = jnp.concatenate([unit[:, q * LB : (q + 1) * LB] for q in range(unit.shape[1] // LB)], axis=0)
@@ -115,7 +119,7 @@
         tokens = lax.dot_general(unit, w_in_ref[...], (((0,), (0,)), ((), ())), preferred_element_type=F32)
         tokens += jnp.concatenate([pos_ref[at, :] for at in places], axis=0).astype(F32)
         square_mean = jnp.mean(tokens * tokens, axis=-1, keepdims=True)
-        normed = (tokens * lax.rsqrt(square_mean + 1e-06) * gain_ref[...]).astype(BF16)
+        normed = (tokens * lax.rsqrt(square_mean + 1e-06) * gain_ref[...].reshape(1, width)).astype(BF16)
         token_sum += jnp.sum(tokens, axis=0, keepdims=True)
         for n, at in enumerate(places):
             tokens_ref[at, :] = tokens[n * LB : (n + 1) * LB]
@@ -158,7 +162,7 @@
 
     def attend(b, heads_sum):
         at = pl.ds(pl.multiple_of(b * LB, LB), LB)
-        chosen = [pattern_ref[b, j] for j in range(KSEL)]
+        chosen = [pattern_ref[0, 0, 0, b, j] for j in range(KSEL)]
         parts = []
         for p in range(PAIRS):
             part = slice(p * LB, (p + 1) * LB)
@@ -226,7 +230,7 @@
 
 def loss_kernel(sizes, place_ref, scale_ref, target_ref, first_ref, own_ref, second_ref, *refs):
     nfreq, nsy, nsx, held = sizes
-    optical_refs, (embed_ref, loss_ref) = refs[:nsx], refs[nsx:]
+    optical_refs, (embed_ref, loss_ref) = refs[:-2], refs[-2:]
     mixed = first_ref[...] + own_ref[...] + second_ref[...]
     embed_ref[...] = mixed
     unit = (mixed * lax.rsqrt(jnp.sum(mixed * mixed) + 1e-06)).astype(BF16)
@@ -246,7 +250,7 @@
         parts.append(logits)
     logits = jnp.concatenate(parts, axis=1) * scale_ref[0]
     place = lax.broadcasted_iota(jnp.int32, logits.shape, 1)
-    logits = jnp.where(jnp.concatenate([first] * nsx, axis=1), logits, -jnp.inf)
+    logits = jnp.where(jnp.concatenate([first] * len(parts), axis=1), logits, -jnp.inf)
     highest = jnp.max(logits, axis=1, keepdims=True)
     summed = jnp.sum(jnp.exp(logits - highest), axis=1, keepdims=True)
 
@@ -256,11 +260,12 @@
     device = target // held
     sx = (place_ref[2] - device) & (nsx - 1)
     sy = (device // nsx) % nsy
-    sy = (((place_ref[1] >> 1) - (sy >> 1)) & (nsy // 2 - 1)) * 2 + ((place_ref[1] ^ sy) & 1)
+    core = (place_ref[1] ^ sy) & 1
+    sy = ((place_ref[1] >> 1) - (sy >> 1)) & (nsy // 2 - 1)
     f = device // (nsx * nsy)
     flipped = jnp.where((f ^ place_ref[0]) & half != 0, 1, 0)
     y = (place_ref[0] - f) & (half - 1)
-    where = ((((sx * 2 + flipped) * half + y) * nsy + sy) * quarters) * held + k
+    where = (((((core * nsx + sx) * 2 + flipped) * half + y) * (nsy // 2) + sy) * quarters) * held + k
     positive = jnp.sum(jnp.where(place == where, logits, 0.0), axis=1, keepdims=True)
     loss_ref[...] = jnp.log(summed) + highest - positive
 
@@ -297,7 +302,7 @@
         out_specs=(VMEM,) * 5,
         compiler_params=vmem(32),
         cost_estimate=pl.CostEstimate(flops=8_000_000_000, bytes_accessed=12_000_000, transcendentals=1_000_000),
-    )(place, *pieces, norm_gain.reshape(1, width), *weights)
+    )(place, *pieces, norm_gain, *weights)
 
 
 def attend(choose, attn_scale, queries, keys, values, token_sum, w_out, w_proj):
@@ -347,22 +352,28 @@
         return lax.ppermute(array, "freq", [(i, (i + half) % nfreq) for i in range(nfreq)])
 
     blocks = jax.ShapeDtypeStruct((half, pixels, local_chans), BF16)
-    near, far, unit = pl.pallas_call(
+    near, far = pl.pallas_call(
         pack_kernel,
-        out_shape=(blocks, blocks, jax.ShapeDtypeStruct((rows, LB), BF16)),
-        in_specs=[SMEM, VMEM, VMEM],
-        out_specs=(VMEM,) * 3,
+        out_shape=(blocks, blocks),
+        in_specs=[SMEM, VMEM],
+        out_specs=(VMEM,) * 2,
         scratch_shapes=[pltpu.VMEM((local_chans * side, cube.shape[2]), F32)],
         compiler_params=vmem(8),
-    )(place, cube, optical)
+    )(place, cube)
+    unit = pl.pallas_call(
+        unit_kernel,
+        out_shape=jax.ShapeDtypeStruct((rows, LB), BF16),
+        in_specs=[VMEM] * 2,
+        out_specs=VMEM,
+        compiler_params=vmem(4),
+    )(near, optical)
     far = other_half(far)
-    unit = jnp.concatenate([unit, lax.ppermute(unit, "sy", [(i, i ^ 1) for i in range(nsy)])], axis=0)
     units = [unit] + [lax.ppermute(unit, "sy", [(i, (i + 2 * d) % nsy) for i in range(nsy)]) for d in range(1, nsy // 2)]
     far, *weights = lax.optimization_barrier((far, pos_embed, w_in, w_query, w_key, w_value))
     weights = load((False, False, False, True, False), *weights)
     sent = pl.pallas_call(
         merge_kernel,
-        out_shape=(jax.ShapeDtypeStruct((2 * pixels + nsy * rows, LB), BF16),) * (half - 1),
+        out_shape=(jax.ShapeDtypeStruct((2 * pixels + nsy // 2 * rows, LB), BF16),) * (half - 1),
         in_specs=[VMEM] * (2 + len(units)),
         out_specs=(VMEM,) * (half - 1),
         compiler_params=vmem(8),
@@ -371,13 +382,11 @@
     candidates = jnp.concatenate(units + [array[2 * pixels :] for array in taken], axis=0)
     others = other_half(candidates)
     tokens, queries, keys, values, token_sum = project(place, [near, far] + taken, norm_gain, weights)
-    others, token_sum = lax.optimization_barrier((others, token_sum))
     candidates = jnp.concatenate([candidates, others], axis=0)
     candidates = [candidates] + [
         lax.ppermute(candidates, "sx", [(i, (i + d) % nsx) for i in range(nsx)]) for d in range(1, nsx)
     ]
-    choose = pattern.reshape(pattern.shape[3], pattern.shape[4])
-    heads_out, proj, held_out = attend(choose, attn_scale, queries, keys, values, token_sum, w_out, w_proj)
+    heads_out, proj, held_out = attend(pattern, attn_scale, queries, keys, values, token_sum, w_out, w_proj)
     layer_out, done = pl.pallas_call(
         layer_kernel,
         out_shape=(jax.ShapeDtypeStruct(tokens.shape, BF16), jax.ShapeDtypeStruct((8, LB), F32)),
@@ -387,7 +396,6 @@
         compiler_params=vmem(16),
         cost_estimate=pl.CostEstimate(flops=2_000_000_000, bytes_accessed=8_000_000, transcendentals=0),
     )(tokens, heads_out, held_out)
-
     even = lax.ppermute(proj, ("freq", "sx"), column_pairs(0, nfreq, nsx))
     odd = lax.ppermute(proj, ("freq", "sx"), column_pairs(1, nfreq, nsx))
     line = jax.ShapeDtypeStruct((1, width), F32)
@@ -398,12 +406,16 @@
         out_specs=(VMEM,) * 3,
         compiler_params=vmem(4),
     )(place, proj, even, odd, mix_weight, done)
+    own, *candidates = lax.optimization_barrier((own, *candidates))
+    candidates = jnp.concatenate(candidates, axis=0)
+    candidates = [candidates, lax.ppermute(candidates, "sy", pairs(nsy, 0))]
+
     first = lax.ppermute(first, "sy", pairs(nsy, 0))
     second = lax.ppermute(second, "sy", pairs(nsy, 1))
     embed, loss = pl.pallas_call(
         functools.partial(loss_kernel, (nfreq, nsy, nsx, held)),
         out_shape=(line, jax.ShapeDtypeStruct((1, 1), F32)),
-        in_specs=[SMEM] * 3 + [VMEM] * (3 + nsx),
+        in_specs=[SMEM] * 3 + [VMEM] * (3 + len(candidates)),
         out_specs=(VMEM, VMEM),
         compiler_params=vmem(8),
     )(place, logit_scale, match_ids.reshape(1), first, own, second, *candidates)

time: 80.2 us -> 75 us (0.935)
  waiting for transfers between devices: 12 us -> 8.19 us
  starting transfers between devices: 37.8 us -> 36.3 us
    ppermute x1, starting transfers between devices: 6.39 us -> 0.1 us  [per_device(): first = lax.ppermute(first, 'sy', pairs(nsy, 0))]
    ppermute x1, starting transfers between devices: 0.76 us -> 4.87 us  [per_device(): candidates = [candidates, lax.ppermute(candidates, 'sy', pairs(nsy, 0))]]
    ppermute x2, waiting for transfers between devices: 1.82 us -> 0.01 us  [other_half(): lax.ppermute(array, 'freq', [(i, (i + half) % nfreq) for i in range(nfreq)])]
    ppermute x1, waiting for transfers between devices: 1.5 us -> 0.01 us  [per_device(): odd = lax.ppermute(proj, ('freq', 'sx'), column_pairs(1, nfreq, nsx))]
    reshape x2 -> x0, local copies, waits for them, and re-layouts: 1.44 us -> none  [the longest x1 0.75 us: per_device(): choose = pattern.reshape(pattern.shape[3], pattern.shape[4])]
    ppermute x3, waiting for transfers between devices: 0.01 us -> 0.97 us  [per_device(): lax.ppermute(candidates, 'sx', [(i, (i + d) % nsx) for i in range(nsx)])]
    ppermute x3, waiting for transfers between devices: 8.08 us -> 7.17 us  [per_device(): lax.ppermute(unit, 'sy', [(i, (i + 2 * d) % nsy) for i in range(nsy)])]
    unnamed x30 -> x34, local copies, waits for them, and re-layouts: 6.86 us -> 7.63 us
  transfers between devices with their start and end apart: 16 -> 16, of which waited for: 5 -> 3; matrix products, arithmetic and copies ran while one was open for 2% -> 1% of each run, Pallas kernels for 21% -> 22%
where the time goes in v3:
time: 75 us; the launch traced here: 73.8 us
  starting transfers between devices  36.3 us (48%)
  Pallas kernels  19.5 us (26%)
  waiting for transfers between devices  8.19 us (11%)
  local copies, waits for them, and re-layouts  7.67 us (10%)
  between operations  2.17 us (3%)
    ppermute x2, starting transfers between devices, other_half(): lax.ppermute(array, 'freq', [(i, (i + half) % nfreq) for i in range(nfreq)])  7.63 us
    unnamed x34, local copies, waits for them, and re-layouts  7.63 us
    ppermute x3, waiting for transfers between devices, per_device(): lax.ppermute(unit, 'sy', [(i, (i + 2 * d) % nsy) for i in range(nsy)])  7.17 us
    ppermute x1, starting transfers between devices, per_device(): odd = lax.ppermute(proj, ('freq', 'sx'), column_pairs(1, nfreq, nsx))  6.7 us
    pallas_call x1, Pallas kernels, attend(): pl.pallas_call(attend_kernel, out_shape=(jax.ShapeDtypeStruct((chans, wid...  6.68 us
    pallas_call x1, Pallas kernels, project(): pl.pallas_call(project_kernel, out_shape=(jax.ShapeDtypeStruct((chans, wi...  5.67 us
    ppermute x3, starting transfers between devices, steps_y(): lax.ppermute(array, 'freq', [(i, i // half * half + (i + d) % half) for i...  5.06 us
    ppermute x1, starting transfers between devices, per_device(): candidates = [candidates, lax.ppermute(candidates, 'sy', pairs(nsy, 0))]  4.87 us
  transfers between devices with their start and end apart: 16, of which 3 were waited for; matrix products, arithmetic and copies ran while one was open for 1% of the time, Pallas kernels for 22%

profile of v3, /device:TPU:3, one launch (start us, length us, event | category | flops | bytes accessed | tf_op | source)
XLA Modules:
  0.0 73.8 jit_solution(2859139381841498565)
XLA Ops:
  0.7 1.1 %copy-done.4 = bf16[128,16,128]{2,1,0:T(8,128)(2,1)S(1)} copy-done((bf16[128,16,128]{2,1,0:T(8,128)(2,1)S(1)}, bf16[128,16,128]{2,1,0:T(8,128)(2,1)}, u32[]{:S(2)}) %copy-start.4) | copy-done | bytes 524312
  1.8 1.0 %shard_map.166 = (bf16[4,256,128]{2,1,0:T(8,128)(2,1)S(1)}, bf16[4,256,128]{2,1,0:T(8,128)(2,1)S(1)}) custom-call(s32[3]{0:T(128)S(1)} %pad_add_fusion.place_ref, bf16[128,16,128]{2,1,0:T(8,128)(2,1)S(1)} %copy-done.4), custom_call_target="tpu_custom_call" | custom-call | tf_op jit(solution)/shard_map/pallas_call | solution.py:355
  2.8 7.0 %collective-permute-start = (bf16[4,256,128]{2,1,0:T(8,128)(2,1)S(1)}, bf16[4,256,128]{2,1,0:T(8,128)(2,1)S(1)}, u32[]{:S(2)}, u32[]{:S(2)}) collective-permute-start(bf16[4,256,128]{2,1,0:T(8,128)(2,1)S(1)} %get-tuple-element.40), channel_id=1, source_target_pairs={{0,128},{32,160},{64,192},{96,224},{128,0},{160,32},{192,64},{224,... | collective-permute-start | bytes 786440 | tf_op jit(solution)/shard_map/ppermute | solution.py:352
  9.8 0.7 copy-done.7
  10.6 0.7 %collective-permute-start.1 = (bf16[16,128]{1,0:T(8,128)(2,1)S(1)}, bf16[16,128]{1,0:T(8,128)(2,1)S(1)}, u32[]{:S(2)}, u32[]{:S(2)}) collective-permute-start(bf16[16,128]{1,0:T(8,128)(2,1)S(1)} %shard_map.167.refs_0_), channel_id=1, source_target_pairs={{0,8},{4,12},{8,16},{12,20},{16,24},{20,28},{24,0},{28,4},{1,9},{5... | collective-permute-start | bytes 12296 | tf_op jit(solution)/shard_map/ppermute | solution.py:371
  11.4 1.2 %collective-permute-start.2 = (bf16[16,128]{1,0:T(8,128)(2,1)S(1)}, bf16[16,128]{1,0:T(8,128)(2,1)S(1)}, u32[]{:S(2)}, u32[]{:S(2)}) collective-permute-start(bf16[16,128]{1,0:T(8,128)(2,1)S(1)} %shard_map.167.refs_0_), channel_id=1, source_target_pairs={{0,16},{4,20},{8,24},{12,28},{16,0},{20,4},{24,8},{28,12},{1,17},{... | collective-permute-start | bytes 12296 | tf_op jit(solution)/shard_map/ppermute | solution.py:371
  12.6 1.6 %collective-permute-start.3 = (bf16[16,128]{1,0:T(8,128)(2,1)S(1)}, bf16[16,128]{1,0:T(8,128)(2,1)S(1)}, u32[]{:S(2)}, u32[]{:S(2)}) collective-permute-start(bf16[16,128]{1,0:T(8,128)(2,1)S(1)} %shard_map.167.refs_0_), channel_id=1, source_target_pairs={{0,24},{4,28},{8,0},{12,4},{16,8},{20,12},{24,16},{28,20},{1,25},{... | collective-permute-start | bytes 12296 | tf_op jit(solution)/shard_map/ppermute | solution.py:371
  14.2 0.8 %copy.18.pattern_ref = s32[1,1,1,8,3]{4,3,2,1,0:T(8,128)S(1)} copy(s32[1,1,1,8,3]{3,2,4,1,0:T(1,128)} %param.28) | data formatting | bytes 192 | tf_op args[13]
  14.9 6.3 %collective-permute-done.1.refs_1_ = bf16[16,128]{1,0:T(8,128)(2,1)S(1)} collective-permute-done((bf16[16,128]{1,0:T(8,128)(2,1)S(1)}, bf16[16,128]{1,0:T(8,128)(2,1)S(1)}, u32[]{:S(2)}, u32[]{:S(2)}) %collective-permute-start.1) | collective-permute-done | bytes 4128 | tf_op jit(solution)/shard_map/ppermute | solution.py:371
  21.3 0.8 %collective-permute-done.3.refs_3_ = bf16[16,128]{1,0:T(8,128)(2,1)S(1)} collective-permute-done((bf16[16,128]{1,0:T(8,128)(2,1)S(1)}, bf16[16,128]{1,0:T(8,128)(2,1)S(1)}, u32[]{:S(2)}, u32[]{:S(2)}) %collective-permute-start.3) | collective-permute-done | bytes 4128 | tf_op jit(solution)/shard_map/ppermute | solution.py:371
  22.2 1.4 %collective-permute-start.4 = (bf16[576,128]{1,0:T(8,128)(2,1)S(1)}, bf16[576,128]{1,0:T(8,128)(2,1)S(1)}, u32[]{:S(2)}, u32[]{:S(2)}) collective-permute-start(bf16[576,128]{1,0:T(8,128)(2,1)S(1)} %get-tuple-element.42), channel_id=1, source_target_pairs={{0,32},{32,64},{64,96},{96,0},{128,160},{160,192},{192,224},{224,1... | collective-permute-start | bytes 442376 | tf_op jit(solution)/shard_map/ppermute | solution.py:349
  23.5 2.6 %collective-permute-start.5 = (bf16[576,128]{1,0:T(8,128)(2,1)S(1)}, bf16[576,128]{1,0:T(8,128)(2,1)S(1)}, u32[]{:S(2)}, u32[]{:S(2)}) collective-permute-start(bf16[576,128]{1,0:T(8,128)(2,1)S(1)} %get-tuple-element.43), channel_id=1, source_target_pairs={{0,64},{32,96},{64,0},{96,32},{128,192},{160,224},{192,128},{224,1... | collective-permute-start | bytes 442376 | tf_op jit(solution)/shard_map/ppermute | solution.py:349
  26.2 1.1 %collective-permute-start.6 = (bf16[576,128]{1,0:T(8,128)(2,1)S(1)}, bf16[576,128]{1,0:T(8,128)(2,1)S(1)}, u32[]{:S(2)}, u32[]{:S(2)}) collective-permute-start(bf16[576,128]{1,0:T(8,128)(2,1)S(1)} %get-tuple-element.44), channel_id=1, source_target_pairs={{0,96},{32,0},{64,32},{96,64},{128,224},{160,128},{192,160},{224,1... | collective-permute-start | bytes 442376 | tf_op jit(solution)/shard_map/ppermute | solution.py:349
  27.2 1.4 %copy-done = bf16[1024,768]{1,0:T(8,128)(2,1)S(1)} copy-done((bf16[1024,768]{1,0:T(8,128)(2,1)S(1)}, bf16[1024,768]{1,0:T(8,128)(2,1)}, u32[]{:S(2)}) %copy-start) | copy-done | bytes 1572888
  28.6 1.3 %copy-done.2 = bf16[768,768]{1,0:T(8,128)(2,1)S(1)} copy-done((bf16[768,768]{1,0:T(8,128)(2,1)S(1)}, bf16[768,768]{1,0:T(8,128)(2,1)}, u32[]{:S(2)}) %copy-start.2) | copy-done | bytes 1179672
  29.9 1.3 %copy-done.3 = bf16[768,768]{1,0:T(8,128)(2,1)S(1)} copy-done((bf16[768,768]{1,0:T(8,128)(2,1)S(1)}, bf16[768,768]{1,0:T(8,128)(2,1)}, u32[]{:S(2)}) %copy-start.3) | copy-done | bytes 1179672
  31.2 1.0 %copy-done.5 = bf16[256,768]{1,0:T(8,128)(2,1)S(1)} copy-done((bf16[256,768]{1,0:T(8,128)(2,1)S(1)}, bf16[256,768]{1,0:T(8,128)(2,1)}, u32[]{:S(2)}) %copy-start.5) | copy-done | bytes 393240
  32.2 1.4 %shard_map.169 = (bf16[1024,768]{1,0:T(8,128)(2,1)S(1)}, bf16[256,768]{1,0:T(8,128)(2,1)S(1)}, bf16[768,768]{1,0:T(8,128)(2,1)S(1)}, bf16[768,768]{1,0:T(8,128)(2,1)S(1)}, bf16[768,768]{1,0:T(8,128)(2,1)S(1)}) custom-call(bf16[1024,768]{1,0:T(8,128)(2,1)S(1)} %copy-done, bf16[256,768]{1,0:T(8,128)(2,1)S(1)} %copy-done.5, bf16[768,768]{1,0:T(8,128)(2,1)S(1)} %copy-done.1, ...), custom_call_target="tpu_custom_call" | custom-call | bytes 11010048 | tf_op jit(solution)/shard_map/pallas_call | solution.py:278
  33.7 0.6 collective-permute-start.10
  34.3 5.7 %shard_map.170 = (f32[1024,768]{1,0:T(8,128)S(1)}, bf16[1024,768]{1,0:T(8,128)(2,1)S(1)}, bf16[8,768,128]{2,1,0:T(8,128)(2,1)S(1)}, bf16[1024,768]{1,0:T(8,128)(2,1)S(1)}, f32[1,768]{1,0:T(1,128)S(1)}) custom-call(s32[3]{0:T(128)S(1)} %pad_add_fusion.place_ref, bf16[4,256,128]{2,1,0:T(8,128)(2,1)S(1)} %get-tuple-element.39.after_ref.near_ref, ...), custom_call_target="tpu_custom_call" | custom-call | flops 8000000000 | bytes 12000000 | tf_op jit(solution)/shard_map/pallas_call | solution.py:292
  40.0 6.7 %shard_map.171 = (bf16[1024,768]{1,0:T(8,128)(2,1)S(1)}, f32[1,512]{1,0:T(1,128)S(1)}, bf16[768,768]{1,0:T(8,128)(2,1)S(1)}) custom-call(s32[1,1,1,8,3]{4,3,2,1,0:T(8,128)S(1)} %copy.18.pattern_ref, f32[12]{0:T(128)S(1)} %copy-done.11, bf16[1024,768]{1,0:T(8,128)(2,1)S(1)} %get-tuple-element.56.q_ref, bf16[8,768,128]{2,1,0:T(8,128)(2,1)S(1)} %get-tuple-element.57.kt_ref, ...), custom_call_target="tpu_custom_call" | custom-call | flops 8000000000 | bytes 8000000 | tf_op jit(solution)/shard_map/pallas_call | solution.py:310
  46.7 0.5 collective-permute-start.7
  47.2 6.7 %collective-permute-start.8 = (f32[1,512]{1,0:T(1,128)S(1)}, f32[1,512]{1,0:T(1,128)S(1)}, u32[]{:S(2)}, u32[]{:S(2)}) collective-permute-start(f32[1,512]{1,0:T(1,128)S(1)} %get-tuple-element.63.proj_ref), channel_id=1, source_target_pairs={{32,64},{64,32},{96,128},{128,96},{160,192},{192,160},{224,1},{1,2... | collective-permute-start | bytes 6152 | tf_op jit(solution)/shard_map/ppermute | solution.py:400
  54.0 1.3 %collective-permute-start.11 = (bf16[512,128]{1,0:T(8,128)(2,1)S(1)}, bf16[512,128]{1,0:T(8,128)(2,1)S(1)}, u32[]{:S(2)}, u32[]{:S(2)}) collective-permute-start(bf16[512,128]{1,0:T(8,128)(2,1)S(1)} %constant_dynamic-update-slice_fusion.7), channel_id=1, source_target_pairs={{0,1},{1,2},{2,3},{3,0},{4,5},{5,6},{6,7},{7,4},{8,9},{9,10},{10,1... | collective-permute-start | bytes 393224 | tf_op jit(solution)/shard_map/ppermute | solution.py:387
  55.2 1.2 %collective-permute-start.12 = (bf16[512,128]{1,0:T(8,128)(2,1)S(1)}, bf16[512,128]{1,0:T(8,128)(2,1)S(1)}, u32[]{:S(2)}, u32[]{:S(2)}) collective-permute-start(bf16[512,128]{1,0:T(8,128)(2,1)S(1)} %constant_dynamic-update-slice_fusion.7), channel_id=1, source_target_pairs={{0,2},{1,3},{2,0},{3,1},{4,6},{5,7},{6,4},{7,5},{8,10},{9,11},{10,... | collective-permute-start | bytes 393224 | tf_op jit(solution)/shard_map/ppermute | solution.py:387
  56.5 1.8 %collective-permute-start.13 = (bf16[512,128]{1,0:T(8,128)(2,1)S(1)}, bf16[512,128]{1,0:T(8,128)(2,1)S(1)}, u32[]{:S(2)}, u32[]{:S(2)}) collective-permute-start(bf16[512,128]{1,0:T(8,128)(2,1)S(1)} %constant_dynamic-update-slice_fusion.7), channel_id=1, source_target_pairs={{0,3},{1,0},{2,1},{3,2},{4,7},{5,4},{6,5},{7,6},{8,11},{9,8},{10,9... | collective-permute-start | bytes 393224 | tf_op jit(solution)/shard_map/ppermute | solution.py:387
  58.2 2.2 %shard_map.172 = (bf16[1024,768]{1,0:T(8,128)(2,1)}, f32[8,128]{1,0:T(8,128)S(1)}) custom-call(f32[1024,768]{1,0:T(8,128)S(1)} %get-tuple-element.55.tokens_ref, bf16[1024,768]{1,0:T(8,128)(2,1)S(1)} %get-tuple-element.60.heads_ref, bf16[768,768]{1,0:T(8,128)(2,1)S(1)} %get-tuple-element.61.wo_ref), custom_call_target="tpu_custom_call" | custom-call | flops 2000000000 | bytes 8000000 | tf_op jit(solution)/shard_map/pallas_call | solution.py:390
  60.5 0.6 shard_map.173
  61.0 1.0 %collective-permute-done.13 = bf16[512,128]{1,0:T(8,128)(2,1)S(1)} collective-permute-done((bf16[512,128]{1,0:T(8,128)(2,1)S(1)}, bf16[512,128]{1,0:T(8,128)(2,1)S(1)}, u32[]{:S(2)}, u32[]{:S(2)}) %collective-permute-start.13) | collective-permute-done | bytes 131104 | tf_op jit(solution)/shard_map/ppermute | solution.py:387
  62.1 4.9 %collective-permute-start.15 = (bf16[2048,128]{1,0:T(8,128)(2,1)S(1)}, bf16[2048,128]{1,0:T(8,128)(2,1)S(1)}, u32[]{:S(2)}, u32[]{:S(2)}) collective-permute-start(bf16[2048,128]{1,0:T(8,128)(2,1)S(1)} %constant_dynamic-update-slice_fusion.15.refs_0_), channel_id=1, source_target_pairs={{0,4},{4,0},{8,12},{12,8},{16,20},{20,16},{24,28},{28,24},{1,5},{5... | collective-permute-start | bytes 1572872 | tf_op jit(solution)/shard_map/ppermute | solution.py:411
  67.1 3.6 %collective-permute-start.14 = (f32[1,512]{1,0:T(1,128)S(1)}, f32[1,512]{1,0:T(1,128)S(1)}, u32[]{:S(2)}, u32[]{:S(2)}) collective-permute-start(f32[1,512]{1,0:T(1,128)S(1)} %get-tuple-element.68), channel_id=1, source_target_pairs={{4,8},{8,4},{12,16},{16,12},{20,24},{24,20},{5,9},{9,5},{13,17},{1... | collective-permute-start | bytes 6152 | tf_op jit(solution)/shard_map/ppermute | solution.py:414
  72.0 1.9 %shard_map.174 = (f32[1,512]{1,0:T(1,128)}, f32[1,1]{1,0:T(1,128)}) custom-call(s32[3]{0:T(128)S(1)} %pad_add_fusion.place_ref, f32[1]{0:T(128)S(6)} %copy.35.scale_ref, s32[1]{0:T(128)} %bitcast.7.target_ref, f32[1,512]{1,0:T(1,128)S(1)} %collective-permute-done.9.first_ref, f32[1,512]{1,0:T(1,128)S(1)} %get-tuple-element.67.own_ref, ...), custom_call_target="tpu_custom_call" | custom-call | tf_op jit(solution)/shard_map/pallas_call | solution.py:415
  (47 shorter events, 0.5 us)
Async XLA Ops:
  0.6 26.6 %copy-start.1 = (bf16[768,768]{1,0:T(8,128)(2,1)S(1)}, bf16[768,768]{1,0:T(8,128)(2,1)}, u32[]{:S(2)}) copy-start(bf16[768,768]{1,0:T(8,128)(2,1)} %refs_2_) | copy-start | bytes 3538948
  0.7 1.1 %copy-start.4 = (bf16[128,16,128]{2,1,0:T(8,128)(2,1)S(1)}, bf16[128,16,128]{2,1,0:T(8,128)(2,1)}, u32[]{:S(2)}) copy-start(bf16[128,16,128]{2,1,0:T(8,128)(2,1)} %cube_ref.1) | copy-start | bytes 1572868
  2.8 18.4 %collective-permute-start = (bf16[4,256,128]{2,1,0:T(8,128)(2,1)S(1)}, bf16[4,256,128]{2,1,0:T(8,128)(2,1)S(1)}, u32[]{:S(2)}, u32[]{:S(2)}) collective-permute-start(bf16[4,256,128]{2,1,0:T(8,128)(2,1)S(1)} %get-tuple-element.40), channel_id=1, source_target_pairs={{0,128},{32,160},{64,192},{96,224},{128,0},{160,32},{192,64},{224,... | collective-permute-start | bytes 786440 | tf_op jit(solution)/shard_map/ppermute | solution.py:352
  9.8 0.7 copy-start.7
  10.6 10.6 %collective-permute-start.1 = (bf16[16,128]{1,0:T(8,128)(2,1)S(1)}, bf16[16,128]{1,0:T(8,128)(2,1)S(1)}, u32[]{:S(2)}, u32[]{:S(2)}) collective-permute-start(bf16[16,128]{1,0:T(8,128)(2,1)S(1)} %shard_map.167.refs_0_), channel_id=1, source_target_pairs={{0,8},{4,12},{8,16},{12,20},{16,24},{20,28},{24,0},{28,4},{1,9},{5... | collective-permute-start | bytes 12296 | tf_op jit(solution)/shard_map/ppermute | solution.py:371
  11.4 9.9 %collective-permute-start.2 = (bf16[16,128]{1,0:T(8,128)(2,1)S(1)}, bf16[16,128]{1,0:T(8,128)(2,1)S(1)}, u32[]{:S(2)}, u32[]{:S(2)}) collective-permute-start(bf16[16,128]{1,0:T(8,128)(2,1)S(1)} %shard_map.167.refs_0_), channel_id=1, source_target_pairs={{0,16},{4,20},{8,24},{12,28},{16,0},{20,4},{24,8},{28,12},{1,17},{... | collective-permute-start | bytes 12296 | tf_op jit(solution)/shard_map/ppermute | solution.py:371
  12.6 9.6 %collective-permute-start.3 = (bf16[16,128]{1,0:T(8,128)(2,1)S(1)}, bf16[16,128]{1,0:T(8,128)(2,1)S(1)}, u32[]{:S(2)}, u32[]{:S(2)}) collective-permute-start(bf16[16,128]{1,0:T(8,128)(2,1)S(1)} %shard_map.167.refs_0_), channel_id=1, source_target_pairs={{0,24},{4,28},{8,0},{12,4},{16,8},{20,12},{24,16},{28,20},{1,25},{... | collective-permute-start | bytes 12296 | tf_op jit(solution)/shard_map/ppermute | solution.py:371
  22.2 11.5 %collective-permute-start.4 = (bf16[576,128]{1,0:T(8,128)(2,1)S(1)}, bf16[576,128]{1,0:T(8,128)(2,1)S(1)}, u32[]{:S(2)}, u32[]{:S(2)}) collective-permute-start(bf16[576,128]{1,0:T(8,128)(2,1)S(1)} %get-tuple-element.42), channel_id=1, source_target_pairs={{0,32},{32,64},{64,96},{96,0},{128,160},{160,192},{192,224},{224,1... | collective-permute-start | bytes 442376 | tf_op jit(solution)/shard_map/ppermute | solution.py:349
  23.5 10.1 %collective-permute-start.5 = (bf16[576,128]{1,0:T(8,128)(2,1)S(1)}, bf16[576,128]{1,0:T(8,128)(2,1)S(1)}, u32[]{:S(2)}, u32[]{:S(2)}) collective-permute-start(bf16[576,128]{1,0:T(8,128)(2,1)S(1)} %get-tuple-element.43), channel_id=1, source_target_pairs={{0,64},{32,96},{64,0},{96,32},{128,192},{160,224},{192,128},{224,1... | collective-permute-start | bytes 442376 | tf_op jit(solution)/shard_map/ppermute | solution.py:349
  26.2 7.5 %collective-permute-start.6 = (bf16[576,128]{1,0:T(8,128)(2,1)S(1)}, bf16[576,128]{1,0:T(8,128)(2,1)S(1)}, u32[]{:S(2)}, u32[]{:S(2)}) collective-permute-start(bf16[576,128]{1,0:T(8,128)(2,1)S(1)} %get-tuple-element.44), channel_id=1, source_target_pairs={{0,96},{32,0},{64,32},{96,64},{128,224},{160,128},{192,160},{224,1... | collective-permute-start | bytes 442376 | tf_op jit(solution)/shard_map/ppermute | solution.py:349
  27.2 1.4 %copy-start = (bf16[1024,768]{1,0:T(8,128)(2,1)S(1)}, bf16[1024,768]{1,0:T(8,128)(2,1)}, u32[]{:S(2)}) copy-start(bf16[1024,768]{1,0:T(8,128)(2,1)} %refs_0_) | copy-start | bytes 4718596
  28.6 1.3 %copy-start.2 = (bf16[768,768]{1,0:T(8,128)(2,1)S(1)}, bf16[768,768]{1,0:T(8,128)(2,1)}, u32[]{:S(2)}) copy-start(bf16[768,768]{1,0:T(8,128)(2,1)} %refs_3_) | copy-start | bytes 3538948
  29.9 1.3 %copy-start.3 = (bf16[768,768]{1,0:T(8,128)(2,1)S(1)}, bf16[768,768]{1,0:T(8,128)(2,1)}, u32[]{:S(2)}) copy-start(bf16[768,768]{1,0:T(8,128)(2,1)} %refs_4_) | copy-start | bytes 3538948
  31.2 1.0 %copy-start.5 = (bf16[256,768]{1,0:T(8,128)(2,1)S(1)}, bf16[256,768]{1,0:T(8,128)(2,1)}, u32[]{:S(2)}) copy-start(bf16[256,768]{1,0:T(8,128)(2,1)} %refs_1_) | copy-start | bytes 1179652
  32.2 2.1 %copy-start.10 = (f32[768]{0:T(1024)S(1)}, f32[768]{0:T(1024)}, u32[]{:S(2)}) copy-start(f32[768]{0:T(1024)} %gain_ref.1) | copy-start | bytes 9220
  33.7 20.2 %collective-permute-start.10 = (bf16[256,128]{1,0:T(8,128)(2,1)S(1)}, bf16[256,128]{1,0:T(8,128)(2,1)S(1)}, u32[]{:S(2)}, u32[]{:S(2)}) collective-permute-start(bf16[256,128]{1,0:T(8,128)(2,1)S(1)} %get-tuple-element.75), channel_id=1, source_target_pairs={{0,128},{32,160},{64,192},{96,224},{128,0},{160,32},{192,64},{224,... | collective-permute-start | bytes 196616 | tf_op jit(solution)/shard_map/ppermute | solution.py:352
  34.3 5.7 %copy-start.8 = (bf16[768,768]{1,0:T(8,128)(2,1)S(1)}, bf16[768,768]{1,0:T(8,128)(2,1)}, u32[]{:S(2)}) copy-start(bf16[768,768]{1,0:T(8,128)(2,1)} %wo_hbm.1) | copy-start | bytes 3538948
  34.3 5.7 %copy-start.9 = (bf16[768,512]{1,0:T(8,128)(2,1)S(1)}, bf16[768,512]{1,0:T(8,128)(2,1)}, u32[]{:S(2)}) copy-start(bf16[768,512]{1,0:T(8,128)(2,1)} %wproj_hbm.1) | copy-start | bytes 2359300
  34.3 5.7 %copy-start.11 = (f32[12]{0:T(128)S(1)}, f32[12]{0:T(128)}, u32[]{:S(2)}) copy-start(f32[12]{0:T(128)} %scale_ref.2) | copy-start | bytes 148
  46.7 13.7 %collective-permute-start.7 = (f32[1,512]{1,0:T(1,128)S(1)}, f32[1,512]{1,0:T(1,128)S(1)}, u32[]{:S(2)}, u32[]{:S(2)}) collective-permute-start(f32[1,512]{1,0:T(1,128)S(1)} %get-tuple-element.63.proj_ref), channel_id=1, source_target_pairs={{0,32},{32,0},{64,96},{96,64},{128,160},{160,128},{192,224},{224,1... | collective-permute-start | bytes 6152 | tf_op jit(solution)/shard_map/ppermute | solution.py:399
  47.2 13.2 %collective-permute-start.8 = (f32[1,512]{1,0:T(1,128)S(1)}, f32[1,512]{1,0:T(1,128)S(1)}, u32[]{:S(2)}, u32[]{:S(2)}) collective-permute-start(f32[1,512]{1,0:T(1,128)S(1)} %get-tuple-element.63.proj_ref), channel_id=1, source_target_pairs={{32,64},{64,32},{96,128},{128,96},{160,192},{192,160},{224,1},{1,2... | collective-permute-start | bytes 6152 | tf_op jit(solution)/shard_map/ppermute | solution.py:400
  54.0 7.1 %collective-permute-start.11 = (bf16[512,128]{1,0:T(8,128)(2,1)S(1)}, bf16[512,128]{1,0:T(8,128)(2,1)S(1)}, u32[]{:S(2)}, u32[]{:S(2)}) collective-permute-start(bf16[512,128]{1,0:T(8,128)(2,1)S(1)} %constant_dynamic-update-slice_fusion.7), channel_id=1, source_target_pairs={{0,1},{1,2},{2,3},{3,0},{4,5},{5,6},{6,7},{7,4},{8,9},{9,10},{10,1... | collective-permute-start | bytes 393224 | tf_op jit(solution)/shard_map/ppermute | solution.py:387
  55.2 5.8 %collective-permute-start.12 = (bf16[512,128]{1,0:T(8,128)(2,1)S(1)}, bf16[512,128]{1,0:T(8,128)(2,1)S(1)}, u32[]{:S(2)}, u32[]{:S(2)}) collective-permute-start(bf16[512,128]{1,0:T(8,128)(2,1)S(1)} %constant_dynamic-update-slice_fusion.7), channel_id=1, source_target_pairs={{0,2},{1,3},{2,0},{3,1},{4,6},{5,7},{6,4},{7,5},{8,10},{9,11},{10,... | collective-permute-start | bytes 393224 | tf_op jit(solution)/shard_map/ppermute | solution.py:387
  56.5 5.5 %collective-permute-start.13 = (bf16[512,128]{1,0:T(8,128)(2,1)S(1)}, bf16[512,128]{1,0:T(8,128)(2,1)S(1)}, u32[]{:S(2)}, u32[]{:S(2)}) collective-permute-start(bf16[512,128]{1,0:T(8,128)(2,1)S(1)} %constant_dynamic-update-slice_fusion.7), channel_id=1, source_target_pairs={{0,3},{1,0},{2,1},{3,2},{4,7},{5,4},{6,5},{7,6},{8,11},{9,8},{10,9... | collective-permute-start | bytes 393224 | tf_op jit(solution)/shard_map/ppermute | solution.py:387
  58.2 2.2 %copy-start.6 = (f32[3,3,512]{2,1,0:T(4,128)S(1)}, f32[3,3,512]{2,1,0:T(4,128)}, u32[]{:S(2)}) copy-start(f32[3,3,512]{2,1,0:T(4,128)} %mix_ref.1) | copy-start | bytes 55300
  62.1 9.9 %collective-permute-start.15 = (bf16[2048,128]{1,0:T(8,128)(2,1)S(1)}, bf16[2048,128]{1,0:T(8,128)(2,1)S(1)}, u32[]{:S(2)}, u32[]{:S(2)}) collective-permute-start(bf16[2048,128]{1,0:T(8,128)(2,1)S(1)} %constant_dynamic-update-slice_fusion.15.refs_0_), channel_id=1, source_target_pairs={{0,4},{4,0},{8,12},{12,8},{16,20},{20,16},{24,28},{28,24},{1,5},{5... | collective-permute-start | bytes 1572872 | tf_op jit(solution)/shard_map/ppermute | solution.py:411
  67.0 5.0 %collective-permute-start.9 = (f32[1,512]{1,0:T(1,128)S(1)}, f32[1,512]{1,0:T(1,128)S(1)}, u32[]{:S(2)}, u32[]{:S(2)}) collective-permute-start(f32[1,512]{1,0:T(1,128)S(1)} %get-tuple-element.65), channel_id=1, source_target_pairs={{0,4},{4,0},{8,12},{12,8},{16,20},{20,16},{24,28},{28,24},{1,5},{5... | collective-permute-start | bytes 6152 | tf_op jit(solution)/shard_map/ppermute | solution.py:413
  67.1 4.9 %collective-permute-start.14 = (f32[1,512]{1,0:T(1,128)S(1)}, f32[1,512]{1,0:T(1,128)S(1)}, u32[]{:S(2)}, u32[]{:S(2)}) collective-permute-start(f32[1,512]{1,0:T(1,128)S(1)} %get-tuple-element.68), channel_id=1, source_target_pairs={{4,8},{8,4},{12,16},{16,12},{20,24},{24,20},{5,9},{9,5},{13,17},{1... | collective-permute-start | bytes 6152 | tf_op jit(solution)/shard_map/ppermute | solution.py:414
